TPU v7x, 512 devices: a whole 4x4x16 slice. The times are simulated.
512 devices in a mesh: tpl: 8 (over y, core), sta: 64 (over x, z).
Axes of the slice: x: 4, y: 4, z: 16, core: 2. Of those that a mesh axis runs over, the one named last changes fastest.
Arguments:
- samples: bfloat16 [1024, 3, 1152], P('sta', None, 'tpl'), may hold values from -6 to 6
- templates: bfloat16 [2048, 20, 3, 384], P(('tpl', 'sta')), may hold values from -6 to 6
- station_list: int32 [2048, 20], P(('tpl', 'sta')), may hold values from 0 to 1023, as said below
- station_count: int32 [2048], P(('tpl', 'sta')), may hold values from 10 to 20
- moveout: int32 [2048, 20], P(('tpl', 'sta')), may hold values from 0 to 287
- offsets: int32 [1024], replicated, may hold values from 0 to 95
Outputs:
- detection: float32 [2048, 384], P(('tpl', 'sta'))
Inputs may be any that keep to these rules, and one draw needn't show every extreme that they name: `station_list`: A device's templates are 4 consecutive ones. Over all 20 entries of one device's templates, at most 2 fall in one block of 16 consecutive stations, and in every device some block holds exactly 2 of them, all among the first 2 entries of its first template. The entries of one template are distinct.
All inputs are finite; a program needn't handle non-finite values.
Results may differ from a plain program's by a relative error of at most 0.012.
Values may be sent and summed in bfloat16 or wider, within the bound.
A program may use at most 64 MiB of HBM per device.

v0:
```python
import math

import jax
import jax.numpy as jnp
from jax import lax
from jax.sharding import PartitionSpec as P

EPSILON = 1e-06


def tables(length, frame_len):
    row_idx = lax.broadcasted_iota(jnp.int32, (frame_len, frame_len), 0)
    col_idx = lax.broadcasted_iota(jnp.int32, (frame_len, frame_len), 1)
    angles = (row_idx * col_idx % frame_len).astype(jnp.float32) * (2.0 * math.pi / frame_len)
    cosine = jnp.cos(angles)
    sines = jnp.sin(angles)
    forward = jnp.concatenate([cosine, -sines], axis=1).astype(jnp.bfloat16)
    inverse = jnp.concatenate([cosine[:, :length], -sines[:, :length]], axis=0).astype(jnp.bfloat16)
    row_band = lax.broadcasted_iota(jnp.int32, (frame_len, length), 0)
    col_band = lax.broadcasted_iota(jnp.int32, (frame_len, length), 1)
    band = ((row_band >= col_band) & (row_band < col_band + length)).astype(jnp.bfloat16)
    return (forward, inverse, band)


def frame_blocks(rows, length, block_count):
    frames = [rows[:, b * length : (b + 2) * length] for b in range(block_count)]
    return jnp.stack(frames, axis=0)


def block_spectra(blocks, forward):
    flat_rows = blocks.reshape(-1, blocks.shape[-1])
    result = jnp.dot(flat_rows, forward, preferred_element_type=jnp.float32).astype(jnp.bfloat16)
    return result.reshape(blocks.shape[:-1] + (forward.shape[1],))


def block_energy(blocks, band):
    flat_rows = blocks.reshape(-1, blocks.shape[-1])
    squares_f = flat_rows.astype(jnp.float32) ** 2
    high = squares_f.astype(jnp.bfloat16)
    low = (squares_f - lax.optimization_barrier(high).astype(jnp.float32)).astype(jnp.bfloat16)
    windowed = jnp.dot(high, band, preferred_element_type=jnp.float32) + jnp.dot(
        low, band, preferred_element_type=jnp.float32
    )
    return windowed.reshape(blocks.shape[:-1] + (band.shape[1],))


def correlate_rows(data_spec, tmpl_spec, energy, tmpl_power, inverse, length, channels):
    freq_count = data_spec.shape[-1] // 2
    block_count, row_count = (data_spec.shape[0], data_spec.shape[1])
    data_f = data_spec.astype(jnp.float32)
    tmpl_f = tmpl_spec.astype(jnp.float32)[None]
    real_part = (
        tmpl_f[..., :freq_count] * data_f[..., :freq_count]
        + tmpl_f[..., freq_count:] * data_f[..., freq_count:]
    )
    imag_part = (
        tmpl_f[..., :freq_count] * data_f[..., freq_count:]
        - tmpl_f[..., freq_count:] * data_f[..., :freq_count]
    )
    product = jnp.concatenate([real_part, imag_part], axis=-1).astype(jnp.bfloat16)
    lagged = (
        jnp.dot(product.reshape(-1, product.shape[-1]), inverse, preferred_element_type=jnp.float32)
        / freq_count
    )
    lagged = lagged.reshape(block_count, row_count, length)
    scaling = length * jnp.sqrt((energy / length + EPSILON) * (tmpl_power[None, :, None] + EPSILON))
    ratio = (lagged / scaling).reshape(block_count, row_count // channels, channels * length)
    summed = ratio[:, :, :length]
    for comp in range(1, channels):
        summed = summed + ratio[:, :, comp * length : (comp + 1) * length]
    return jnp.transpose(summed, (1, 0, 2)).reshape(row_count // channels, block_count * length)


def stack_all(summed, shifts, alive_mask, out_len):
    lag_idx = lax.broadcasted_iota(jnp.int32, (1, 1, out_len), 2)
    taken = jnp.take_along_axis(summed, lag_idx + shifts[:, :, None], axis=2)
    return jnp.sum(jnp.where(alive_mask[:, :, None], taken, 0.0), axis=1)


def on_device(samples, templates, station_list, station_count, moveout, offsets):
    length = templates.shape[-1]
    channels = templates.shape[2]
    forward, inverse, band = tables(length, 2 * length)
    window = lax.all_gather(samples, "tpl", axis=2, tiled=True)
    owners = lax.axis_size("sta")
    sta_dev = samples.shape[0]
    tpl_dev, list_width = station_list.shape
    capacity = max(2, (3 * tpl_dev * list_width + 2 * owners - 1) // (2 * owners))
    slot_count = owners * capacity
    record_len = window.shape[-1]
    block_count = record_len // length - 1
    out_len = (block_count - 1) * length
    freq_width = 4 * length
    flat_ids = station_list.reshape(-1)
    alive_mask = lax.broadcasted_iota(jnp.int32, station_list.shape, 1) < station_count[:, None]
    live_pairs = alive_mask.reshape(-1)
    owner_of = flat_ids // sta_dev
    local_id = flat_ids % sta_dev
    member = (
        (owner_of[:, None] == jnp.arange(owners, dtype=jnp.int32)[None, :]) & live_pairs[:, None]
    ).astype(jnp.int32)
    before = jnp.cumsum(member, axis=0) - member
    rank_of = jnp.sum(before * member, axis=1)
    slot_of = jnp.where(live_pairs, rank_of * owners + owner_of, 0)
    target = (slot_of[:, None] == jnp.arange(slot_count, dtype=jnp.int32)[None, :]) & live_pairs[
        :, None
    ]
    wanted = jnp.sum(jnp.where(target, local_id[:, None] + 1, 0), axis=0) - 1
    incoming = lax.all_to_all(
        wanted.reshape(capacity, owners), "sta", split_axis=1, concat_axis=1, tiled=True
    )
    incoming_ids = jnp.maximum(incoming, 0)
    offset_of = jnp.sum(
        jnp.where(
            flat_ids[:, None] == jnp.arange(offsets.shape[0], dtype=jnp.int32)[None, :],
            offsets[None, :],
            0,
        ),
        axis=1,
    )
    shifts = (moveout.reshape(-1) + offset_of).reshape(station_list.shape)
    slot_grid = slot_of.reshape(station_list.shape)
    flat_window = window.reshape(sta_dev, channels * record_len)
    arrived = lax.all_to_all(
        flat_window[incoming_ids], "sta", split_axis=1, concat_axis=1, tiled=True
    )
    sample_rows = arrived.reshape(slot_count, channels * record_len)

    def fetch_rows(slot_row):
        rows_here = sample_rows[slot_row].reshape(list_width * channels, record_len)
        blocks_here = frame_blocks(rows_here, length, block_count)
        return (block_spectra(blocks_here, forward), block_energy(blocks_here, band))

    trace_all = templates.reshape(-1, length)
    tmpl_spec = jnp.dot(trace_all, forward[:length], preferred_element_type=jnp.float32).astype(
        jnp.bfloat16
    )
    tmpl_spec = tmpl_spec.reshape(tpl_dev, list_width * channels, freq_width)
    tmpl_power = jnp.mean(trace_all.astype(jnp.float32) ** 2, axis=-1).reshape(
        tpl_dev, list_width * channels
    )

    def per_template(packed):
        slot_row, spec_row, power_row = packed
        spectra_here, energy_here = fetch_rows(slot_row)
        return correlate_rows(
            spectra_here, spec_row, energy_here, power_row, inverse, length, channels
        )

    summed_all = lax.map(per_template, (slot_grid, tmpl_spec, tmpl_power))
    stacked = stack_all(summed_all, shifts, alive_mask, out_len)
    return stacked * lax.rsqrt(jnp.mean(stacked * stacked, axis=-1, keepdims=True) + EPSILON)


def solution(mesh):
    in_specs = (
        P("sta", None, "tpl"),
        P(("tpl", "sta"), None, None, None),
        P(("tpl", "sta"), None),
        P(("tpl", "sta")),
        P(("tpl", "sta"), None),
        P(),
    )
    out_specs = P(("tpl", "sta"), None)
    return jax.shard_map(
        on_device, mesh=mesh, in_specs=in_specs, out_specs=out_specs, check_vma=False
    )
```

profile of v0, /device:TPU:1, one launch (start us, length us, event | category | flops | bytes accessed | tf_op | source)
XLA Modules:
  0.0 462.9 jit_solution(16551428636099088249)
XLA Ops:
  3.1 19.1 %all-to-all-start = ((s32[2,64,1]{0,2,1:T(1,128)}), s32[2,64,1]{0,2,1:T(1,128)S(1)}, u32[]{:S(2)}, u32[]{:S(2)}) async-start(s32[2,64,1]{0,2,1:T(1,128)} %copy.42), calls=%async_computation | async-start | bytes 65536 | tf_op jit(solution)/shard_map/all_to_all | solution.py:109
  23.2 15.1 %all_gather.3 = bf16[16,3,1152]{0,1,2:T(4,128)(2,1)S(1)} all-gather(bf16[16,3,144]{0,1,2:T(4,128)(2,1)S(1)} %copy.40), channel_id=1, replica_groups=mesh['tpl'=8,'sta'=64] {'tpl'}, dimensions={2}, use_global_device_ids=true | all-gather | bytes 124416 | tf_op jit(solution)/shard_map/all_gather | solution.py:84
  38.3 1.2 copy.41
  39.7 1.2 gather_fusion.1
  40.9 1.8 copy.44
  42.7 15.1 %all-to-all-start.1 = ((bf16[2,64,3456]{2,0,1:T(2,128)(2,1)}), bf16[2,64,3456]{2,0,1:T(2,128)(2,1)}, u32[]{:S(2)}, u32[]{:S(2)}) async-start(bf16[2,64,3456]{2,0,1:T(2,128)(2,1)} %copy.44), calls=%async_computation.1 | async-start | bytes 1769472 | tf_op jit(solution)/shard_map/all_to_all | solution.py:124
  58.2 10.1 %negate_convert_fusion = (bf16[768,768]{1,0:T(8,128)(2,1)S(1)}, bf16[768,768]{1,0:T(8,128)(2,1)S(1)}) fusion(), kind=kLoop, calls=%fused_computation.53 | loop fusion | flops 7077888 | bytes 2359296 | tf_op jit(solution)/shard_map/convert.9
  70.3 1.1 reshape.254
  72.4 8.9 %fusion.28 = f32[768,768]{1,0:T(8,128)S(1)} fusion(), kind=kLoop, calls=%fused_computation.58 | loop fusion | flops 5308416 | bytes 2359296 | tf_op jit(solution)/shard_map/sin | solution.py:16
  81.5 1.1 pad_maximum_fusion.2
  83.5 18.4 %all-to-all-done.1 = bf16[2,64,3456]{2,0,1:T(2,128)(2,1)} async-done(((bf16[2,64,3456]{2,0,1:T(2,128)(2,1)}), bf16[2,64,3456]{2,0,1:T(2,128)(2,1)}, u32[]{:S(2)}, u32[]{:S(2)}) %all-to-all-start.1) | async-done | bytes 884768 | tf_op jit(solution)/shard_map/all_to_all | solution.py:124
  101.9 2.2 copy.45
  104.2 55.8 %while.12 = (s32[]{:T(128)}, f32[4,20,768]{2,1,0:T(8,128)S(1)}, bf16[4,60,1536]{2,1,0:T(8,128)(2,1)}, s32[4,20]{1,0:T(4,128)S(1)}, bf16[128,3456]{1,0:T(8,128)(2...) while((s32[]{:T(128)}, f32[4,20,768]{2,1,0:T(8,128)S(1)}, ...), condition=%wide.region_6.7_spmd.clone.clone, body=%wide.region_5.6_spmd.clone.clone.sunk | while | flops 571986048 | bytes 16407181 | solution.py:150
  104.2 2.1 gather_fusion
  107.1 1.4 fusion.74
  110.5 1.3 add_convert_fusion.2
  111.8 2.3 convolution_multiply_fusion.2
  118.1 2.1 gather_fusion
  121.0 1.4 fusion.74
  124.4 1.3 add_convert_fusion.2
  125.8 2.3 convolution_multiply_fusion.2
  129.5 1.1 fusion.77
  132.1 2.1 gather_fusion
  135.0 1.4 fusion.74
  138.4 1.3 add_convert_fusion.2
  139.8 2.3 convolution_multiply_fusion.2
  143.5 1.1 fusion.77
  146.1 2.1 gather_fusion
  149.0 1.4 fusion.74
  152.4 1.3 add_convert_fusion.2
  153.7 2.3 convolution_multiply_fusion.2
  160.0 301.9 %gather_fusion.2 = f32[30720]{0:T(1024)S(1)} fusion(f32[4,20,768]{2,1,0:T(8,128)S(1)} %get-tuple-element.55, s32[30720]{0:T(1024)S(1)} %reshape.277), kind=kCustom, calls=%fused_computation.2 | custom fusion | bytes 614400 | tf_op jit(solution)/shard_map/jit(take_along_axis)/gather | solution.py:76
  (176 shorter events, 34.2 us)
Async XLA Ops:
  1.5 0.5 copy-start.9
  3.1 36.4 %all-to-all-start = ((s32[2,64,1]{0,2,1:T(1,128)}), s32[2,64,1]{0,2,1:T(1,128)S(1)}, u32[]{:S(2)}, u32[]{:S(2)}) async-start(s32[2,64,1]{0,2,1:T(1,128)} %copy.42), calls=%async_computation | async-start | bytes 65536 | tf_op jit(solution)/shard_map/all_to_all | solution.py:109
  40.9 17.0 %copy-start.5 = (bf16[4,20,3,384]{3,0,2,1:T(4,128)(2,1)S(1)}, bf16[4,20,3,384]{3,0,2,1:T(4,128)(2,1)}, u32[]{:S(2)}) copy-start(bf16[4,20,3,384]{3,0,2,1:T(4,128)(2,1)} %param.9) | copy-start | bytes 552964
  42.7 59.2 %all-to-all-start.1 = ((bf16[2,64,3456]{2,0,1:T(2,128)(2,1)}), bf16[2,64,3456]{2,0,1:T(2,128)(2,1)}, u32[]{:S(2)}, u32[]{:S(2)}) async-start(bf16[2,64,3456]{2,0,1:T(2,128)(2,1)} %copy.44), calls=%async_computation.1 | async-start | bytes 1769472 | tf_op jit(solution)/shard_map/all_to_all | solution.py:124
  68.3 1.0 copy-start.1
  68.3 1.4 copy-start.3
  69.7 2.2 copy-start.7
  69.8 2.5 copy-start.8
  70.3 11.0 %copy-start.6 = (s32[4,20]{1,0:T(4,128)S(1)}, s32[4,20]{1,0:T(4,128)}, u32[]{:S(2)}) copy-start(s32[4,20]{1,0:T(4,128)} %param.10) | copy-start | bytes 964
  70.3 11.0 %copy-start.11 = (s32[4]{0:T(128)S(1)}, s32[4]{0:T(128)}, u32[]{:S(2)}) copy-start(s32[4]{0:T(128)} %param.11) | copy-start | bytes 52
  81.3 1.3 copy-start.2
  81.3 2.0 copy-start.4
  110.5 4.7 %copy-start = (bf16[120,768]{1,0:T(8,128)(2,1)S(1)}, bf16[120,768]{1,0:T(8,128)(2,1)}, u32[]{:S(2)}) copy-start(bf16[120,768]{1,0:T(8,128)(2,1)} %reshape.307) | copy-start | bytes 552964 | tf_op jit(solution)/shard_map/while
  124.4 4.7 %copy-start = (bf16[120,768]{1,0:T(8,128)(2,1)S(1)}, bf16[120,768]{1,0:T(8,128)(2,1)}, u32[]{:S(2)}) copy-start(bf16[120,768]{1,0:T(8,128)(2,1)} %reshape.307) | copy-start | bytes 552964 | tf_op jit(solution)/shard_map/while
  138.4 4.7 %copy-start = (bf16[120,768]{1,0:T(8,128)(2,1)S(1)}, bf16[120,768]{1,0:T(8,128)(2,1)}, u32[]{:S(2)}) copy-start(bf16[120,768]{1,0:T(8,128)(2,1)} %reshape.307) | copy-start | bytes 552964 | tf_op jit(solution)/shard_map/while
  152.3 4.7 %copy-start = (bf16[120,768]{1,0:T(8,128)(2,1)S(1)}, bf16[120,768]{1,0:T(8,128)(2,1)}, u32[]{:S(2)}) copy-start(bf16[120,768]{1,0:T(8,128)(2,1)} %reshape.307) | copy-start | bytes 552964 | tf_op jit(solution)/shard_map/while
  160.0 302.0 %copy-start.10 = (pred[4,20]{1,0:T(4,128)(4,1)S(1)}, pred[4,20]{1,0:T(4,128)(4,1)}, u32[]{:S(2)}) copy-start(pred[4,20]{1,0:T(4,128)(4,1)} %copy-done.9) | copy-start | bytes 244
where the time goes:
time: 467 us; the launch traced here: 463 us
  local copies, waits for them, and re-layouts  340 us (73%)
  starting transfers between devices  34.2 us (7%)
  other arithmetic  33 us (7%)
  matrix products  21.1 us (5%)
  waiting for transfers between devices  18.4 us (4%)
  blocking collectives  15.1 us (3%)
    gather x3, local copies, waits for them, and re-layouts, stack_all(): taken = jnp.take_along_axis(summed, lag_idx + shifts[:, :, None], axis=2)  302 us
    all_to_all x1, starting transfers between devices, on_device(): lax.all_to_all(wanted.reshape(capacity, owners), 'sta', split_axis=1, con...  19.1 us
    all_to_all x1, waiting for transfers between devices, on_device(): lax.all_to_all(flat_window[incoming_ids], 'sta', split_axis=1, concat_axi...  18.4 us
    another operation x6, other arithmetic  15.4 us
    all_gather x1, blocking collectives, on_device(): window = lax.all_gather(samples, 'tpl', axis=2, tiled=True)  15.1 us
    all_to_all x1, starting transfers between devices, on_device(): lax.all_to_all(flat_window[incoming_ids], 'sta', split_axis=1, concat_axi...  15.1 us
  transfers between devices with their start and end apart: 2, of which 1 were waited for; matrix products, arithmetic and copies ran while one was open for 6% of the time, Pallas kernels for 0%

commit v1 on v0

v1 whole, which is shorter than its diff:
```python
import functools
import math

import jax
import jax.numpy as jnp
import numpy as np
from jax import lax
from jax.experimental import pallas as pl
from jax.experimental.pallas import tpu as pltpu
from jax.sharding import PartitionSpec as P

EPSILON = 1e-06
LANES = 128
ROWS = 8
CAPACITY = 2
MESH = pl.DeviceIdType.MESH
F32 = jnp.float32
BF16 = jnp.bfloat16


def tables(length):
    frame = 2 * length
    time = np.arange(frame)
    odd = 2 * np.arange(length) + 1
    angles = (np.outer(time, odd) % (2 * frame)).astype(np.float64) * (math.pi / frame)
    cosine, sine = np.cos(angles), np.sin(angles)
    forward = np.concatenate([cosine, -sine], axis=1)
    inverse = np.concatenate([cosine[:length].T, -sine[:length].T], axis=0)
    row = np.arange(frame)[:, None]
    col = np.arange(length)[None, :]
    band = (row >= col) & (row < col + length)
    return tuple(jnp.asarray(a.astype(np.float32), BF16) for a in (forward, inverse, band))


def iota(shape, dim):
    return lax.broadcasted_iota(jnp.int32, shape, dim)


def dot(a, b):
    return jnp.dot(a, b, preferred_element_type=F32)


def split(value):
    high = value.astype(BF16)
    return high, (value - high.astype(F32)).astype(BF16)


def third(value):
    return (value * 171) >> 9


def kernel(
    sizes,
    samples,
    templates,
    station_list,
    station_count,
    moveout,
    offsets,
    forward_hbm,
    inverse_hbm,
    band_hbm,
    out,
    forward,
    inverse,
    band,
    raw,
    traces,
    small,
    pick,
    outbox,
    inbox,
    parts,
    replies,
    answers,
    local_sem,
    part_send,
    part_recv,
    box_sem,
    back_sem,
):
    tpl, sta, stations, channels, tpl_dev, width, length = sizes
    depth = 2 * tpl
    owners = sta
    frame = 2 * length
    rows_all = owners * ROWS
    slots = CAPACITY * owners
    entries = tpl_dev * width * channels
    columns = (entries + LANES - 1) // LANES * LANES

    p = lax.axis_index("tpl")
    s = lax.axis_index("sta")
    x, z = s // depth, s % depth
    slab, half = z // 2, z % 2
    me = x * depth + 2 * p + half

    def member(o):
        return {"tpl": (o % depth) // 2, "sta": (o // depth) * depth + 2 * slab + o % 2}

    def source(i):
        return {"tpl": i, "sta": me}

    def handler(i):
        return {"tpl": slab, "sta": x * depth + 2 * i + half}

    own = jnp.where(s == me, 1, 0)

    load_raw = pltpu.make_async_copy(templates, raw, local_sem.at[0])
    load_forward = pltpu.make_async_copy(forward_hbm, forward, local_sem.at[1])
    load_band = pltpu.make_async_copy(band_hbm, band, local_sem.at[2])
    load_inverse = pltpu.make_async_copy(inverse_hbm, inverse, local_sem.at[3])
    load_raw.start()
    load_forward.start()
    load_band.start()
    load_inverse.start()

    barrier = pltpu.get_barrier_semaphore()

    def greet(i, carry):
        o = lax.rem(me + i, owners)
        pl.semaphore_signal(barrier, inc=1, device_id=member(o), device_id_type=MESH)
        return carry

    lax.fori_loop(1, owners, greet, 0)
    for i in range(tpl):

        @pl.when((s != me) | (p != i))
        def _():
            pl.semaphore_signal(barrier, inc=1, device_id=source(i), device_id_type=MESH)

    small[...] = jnp.zeros(small.shape, F32)
    stations_here = station_list[...]
    moves = moveout[...]
    small[0:tpl_dev, 0:width] = (stations_here >> 4).astype(F32)
    small[8 : 8 + tpl_dev, 0:width] = (stations_here & 15).astype(F32)
    small[16 : 16 + tpl_dev, 0:width] = (moves >> 1).astype(F32)
    small[24 : 24 + tpl_dev, 0:width] = (moves & 1).astype(F32)
    col = iota((ROWS, columns), 1)
    col_tpl = col & 3
    col_key = third(col >> 2)
    col_chan = (col >> 2) - 3 * col_key
    expand_row = iota((LANES, columns), 0)
    expand_key = third(iota((LANES, columns), 1) >> 2)
    expand = jnp.where(expand_row == expand_key, 1.0, 0.0).astype(BF16)
    spread = dot(small[...].astype(BF16), expand)
    mine = iota((ROWS, columns), 0) == col_tpl

    def flat(i):
        return jnp.sum(jnp.where(mine, spread[8 * i : 8 * i + 8], 0.0), axis=0, keepdims=True)

    owner_of, local_id, move_high, move_low = flat(0), flat(1), flat(2), flat(3)
    used = jnp.zeros((ROWS, columns), jnp.int32)
    for t in range(tpl_dev):
        used = jnp.where(col_tpl == t, station_count[t], used)
    live = (col_key < used) & (col < entries)
    owner_live = jnp.where(live[0:1], owner_of, -1.0)

    row = iota((rows_all, 1), 0)
    row_owner = (row >> 3).astype(F32)
    q = row & 7
    row_rank = jnp.where(((q >= 3) & (q < 6)) | (q == 7), 1.0, 0.0)
    row_chan = jnp.where(q >= 6, 0, jnp.where(q >= 3, q - 3, q))
    belongs = owner_live == row_owner
    up_row, up_col = iota((columns, columns), 0), iota((columns, columns), 1)
    up_chan = (up_row >> 2) - 3 * third(up_row >> 2)
    up_chan_col = (up_col >> 2) - 3 * third(up_col >> 2)
    earlier = jnp.where((up_row < up_col) & (up_chan == up_chan_col), 1.0, 0.0).astype(BF16)
    before = dot(jnp.where(belongs, 1.0, 0.0).astype(BF16), earlier)
    hot = jnp.where(
        belongs & (before == row_rank) & (col_chan[0:1] == row_chan), 1.0, 0.0
    )
    pick[...] = hot.astype(BF16)

    load_raw.wait()
    quads = raw[...].astype(F32).reshape(width * channels // 2, 2, tpl_dev, length)
    traces[...] = jnp.zeros(traces.shape, F32)
    traces[0 : width * channels // 2, 0:4, :] = quads[:, 0]
    traces[0 : width * channels // 2, 4:8, :] = quads[:, 1]
    placed = dot(pick[...], traces[...].reshape(columns, length).astype(BF16))
    ones = jnp.ones((columns, LANES), BF16)
    notes = jnp.concatenate(
        [dot((hot * v).astype(BF16), ones) for v in (local_id, move_high, move_low)], axis=1
    )
    outbox[...] = (
        jnp.where(q < 6, placed, notes).reshape(owners, ROWS, length).astype(BF16)
    )

    pl.semaphore_wait(barrier, owners - 1 + tpl - own)

    def part_copy(i):
        return pltpu.make_async_remote_copy(
            src_ref=samples,
            dst_ref=parts.at[p],
            send_sem=part_send.at[i],
            recv_sem=part_recv.at[p],
            device_id=handler(i),
            device_id_type=MESH,
        )

    for i in range(tpl):
        remote = (own == 0) | (slab != i)

        @pl.when(remote)
        def _():
            part_copy(i).start()

        @pl.when(jnp.logical_not(remote))
        def _():
            pltpu.make_async_copy(samples, parts.at[p], part_recv.at[p]).start()

    def box_copy(i):
        o = lax.rem(me + i, owners)
        return pltpu.make_async_remote_copy(
            src_ref=outbox.at[o],
            dst_ref=inbox.at[me],
            send_sem=box_sem.at[0],
            recv_sem=box_sem.at[1],
            device_id=member(o),
            device_id_type=MESH,
        )

    def post(i, carry):
        box_copy(i).start()
        return carry

    keep = pltpu.make_async_copy(outbox.at[me], inbox.at[me], box_sem.at[2])
    keep.start()
    lax.fori_loop(1, owners, post, 0)

    for i in range(tpl):
        pltpu.make_async_copy(samples, parts.at[i], part_recv.at[i]).wait()
    record = jnp.concatenate([parts[i].astype(F32) for i in range(tpl)], axis=1)
    blocks = jnp.concatenate([record[:, :frame], record[:, length : length + frame]], axis=0)
    load_forward.wait()
    spectra = dot(blocks.astype(BF16), forward[...]).astype(BF16)
    load_band.wait()
    high, low = split(blocks * blocks)
    energy = dot(high, band[...]) + dot(low, band[...])
    norm = (2.0 / (frame * length)) * lax.rsqrt(energy * (1.0 / length) + EPSILON)
    norm_high, norm_low = split(norm)
    held = stations * channels

    order_row = iota((rows_all, rows_all), 0)
    order_col = iota((rows_all, rows_all), 1)
    group, sender = order_row // owners, order_row % owners
    place = jnp.where(group < 6, (group >> 1) + 3 * (group & 1), group)
    order = jnp.where(order_col == sender * ROWS + place, 1.0, 0.0).astype(BF16)

    load_inverse.wait()
    keep.wait()
    everyone = pl.ds(0, owners - 1)
    pltpu.make_async_copy(outbox.at[everyone], inbox.at[everyone], box_sem.at[1]).wait()
    arrived = inbox[...].astype(F32).reshape(rows_all, length).astype(BF16)
    sorted_rows = dot(order, arrived)
    meta = sorted_rows[channels * slots :]
    lane = iota((slots, LANES), 1)
    ids = meta[:, 0:LANES].astype(jnp.int32)
    base = me * stations
    offset_rows = iota(offsets.shape, 0)
    offset_row = jnp.sum(
        jnp.where(offset_rows == base // LANES, offsets[...].astype(F32), 0.0),
        axis=0,
        keepdims=True,
    )
    offset_hot = jnp.where(lane == ids + base % LANES, offset_row, 0.0).astype(BF16)
    offset_of = dot(offset_hot, jnp.ones((LANES, LANES), BF16))
    shift = (
        2.0 * meta[:, LANES : 2 * LANES] + meta[:, 2 * LANES : 3 * LANES] + offset_of
    ).astype(jnp.int32)

    sums = [None] * 2
    for c in range(channels):
        trace = sorted_rows[c * slots : (c + 1) * slots]
        power = jnp.sum(trace * trace, axis=1, keepdims=True) * (1.0 / length)
        scale = lax.rsqrt(power + EPSILON)
        tspec = dot(trace.astype(BF16), forward[0:length, :]).astype(BF16).astype(F32)
        y_re, y_im = tspec[:, :length], tspec[:, length:]
        station_hot = jnp.where(
            iota((slots, stations), 1) == ids[:, :stations], 1.0, 0.0
        ).astype(BF16)
        for b in range(2):
            at = slice(b * held + c * stations, b * held + (c + 1) * stations)
            data = dot(station_hot, spectra[at])
            x_re, x_im = data[:, :length], data[:, length:]
            product = jnp.concatenate(
                [y_re * x_re + y_im * x_im, y_re * x_im - y_im * x_re], axis=1
            ).astype(BF16)
            lagged = dot(product, inverse[...])
            weight = dot(station_hot, norm_high[at]) + dot(station_hot, norm_low[at])
            term = lagged * weight * scale
            sums[b] = term if c == 0 else sums[b] + term

    tiles = [
        sums[b][:, j * LANES : (j + 1) * LANES] for b in range(2) for j in range(length // LANES)
    ]
    span = length // LANES
    for bit in (2, 1):
        chosen = (shift & (bit * LANES)) != 0
        tiles = [
            jnp.where(chosen, tiles[min(i + bit, len(tiles) - 1)], tiles[i])
            for i in range(span + bit)
        ]
    step = LANES // 2
    while step >= 1:
        chosen = (shift & step) != 0
        turned = [pltpu.roll(tile, LANES - step, 1) for tile in tiles]
        inside = lane < LANES - step
        after = turned[1:] + turned[-1:]
        tiles = [
            jnp.where(chosen, jnp.where(inside, turned[i], after[i]), tiles[i])
            for i in range(span + 1)
        ]
        step //= 2
    replies[...] = jnp.zeros(replies.shape, F32)
    for r in range(CAPACITY):
        for j in range(span):
            replies[:, r * span + j, :] = tiles[j][r * owners : (r + 1) * owners]

    def reply_copy(i):
        o = lax.rem(me + i, owners)
        return pltpu.make_async_remote_copy(
            src_ref=replies.at[o],
            dst_ref=answers.at[me],
            send_sem=back_sem.at[0],
            recv_sem=back_sem.at[1],
            device_id=member(o),
            device_id_type=MESH,
        )

    def answer(i, carry):
        reply_copy(i).start()
        return carry

    keep_back = pltpu.make_async_copy(replies.at[me], answers.at[me], back_sem.at[2])
    keep_back.start()
    lax.fori_loop(1, owners, answer, 0)

    wide = iota((4 * ROWS, columns), 0)
    wide_col = iota((4 * ROWS, columns), 1)
    of_template = jnp.where((wide & 7) == (wide_col & 3), 1.0, 0.0).astype(BF16)
    weights = lax.dot_general(
        of_template, pick[...], (((1,), (1,)), ((), ())), preferred_element_type=F32
    )
    weight_q = iota((4 * ROWS, rows_all), 1) & 7
    weight_j = iota((4 * ROWS, rows_all), 0) >> 3
    matches = (weight_q < 6) & (
        (weight_q == weight_j) | (weight_q == weight_j + 3)
    )
    weights = jnp.where(matches & (weight_j < 3), weights, 0.0).astype(BF16)

    keep_back.wait()
    pltpu.make_async_copy(replies.at[everyone], answers.at[everyone], back_sem.at[1]).wait()
    high, low = split(answers[...].reshape(rows_all, LANES))
    stacked = dot(weights, high) + dot(weights, low)
    chunks = [stacked[ROWS * j : ROWS * (j + 1)] for j in range(span)]
    square = chunks[0] * chunks[0]
    for chunk in chunks[1:]:
        square = square + chunk * chunk
    mean = jnp.sum(square, axis=1, keepdims=True) * (1.0 / length)
    root = lax.rsqrt(mean + EPSILON)
    for j in range(span):
        out[:, j * LANES : (j + 1) * LANES] = (chunks[j] * root)[:tpl_dev]

    for i in range(tpl):

        @pl.when((own == 0) | (slab != i))
        def _():
            part_copy(i).wait_send()

    pltpu.make_async_copy(outbox.at[everyone], inbox.at[everyone], box_sem.at[0]).wait()
    pltpu.make_async_copy(replies.at[everyone], answers.at[everyone], back_sem.at[0]).wait()


def on_device(samples, templates, station_list, station_count, moveout, offsets):
    stations, channels, part = samples.shape
    tpl_dev, width, _, length = templates.shape
    tpl, sta = lax.axis_size("tpl"), lax.axis_size("sta")
    sizes = (tpl, sta, stations, channels, tpl_dev, width, length)
    rows = jnp.transpose(samples, (1, 0, 2)).reshape(channels * stations, part)
    quads = jnp.transpose(templates, (1, 2, 0, 3)).reshape(width * channels, tpl_dev, length)
    offset_grid = offsets.reshape(-1, LANES)
    frame = 2 * length
    entries = tpl_dev * width * channels
    columns = (entries + LANES - 1) // LANES * LANES
    anywhere = pl.BlockSpec(memory_space=pl.ANY)
    vmem = pl.BlockSpec(memory_space=pltpu.VMEM)
    smem = pl.BlockSpec(memory_space=pltpu.SMEM)
    dma = pltpu.SemaphoreType.DMA
    return pl.pallas_call(
        functools.partial(kernel, sizes),
        out_shape=jax.ShapeDtypeStruct((tpl_dev, length), F32),
        in_specs=[anywhere, anywhere, vmem, smem, vmem, vmem, anywhere, anywhere, anywhere],
        out_specs=vmem,
        scratch_shapes=[
            pltpu.VMEM((frame, frame), BF16),
            pltpu.VMEM((frame, length), BF16),
            pltpu.VMEM((frame, length), BF16),
            pltpu.VMEM((width * channels, tpl_dev, length), BF16),
            pltpu.VMEM((columns // ROWS, ROWS, length), F32),
            pltpu.VMEM((4 * ROWS, LANES), F32),
            pltpu.VMEM((sta * ROWS, columns), BF16),
            pltpu.VMEM((sta, ROWS, length), BF16),
            pltpu.VMEM((sta, ROWS, length), BF16),
            pltpu.VMEM((tpl, channels * stations, part), BF16),
            pltpu.VMEM((sta, ROWS, LANES), F32),
            pltpu.VMEM((sta, ROWS, LANES), F32),
            dma((4,)),
            dma((tpl,)),
            dma((tpl,)),
            dma((3,)),
            dma((3,)),
        ],
        compiler_params=pltpu.CompilerParams(
            collective_id=0, has_side_effects=True, vmem_limit_bytes=48 * 2**20
        ),
        cost_estimate=pl.CostEstimate(
            flops=2 * 10**9, bytes_accessed=6 * 10**6, transcendentals=10**5
        ),
    )(rows, quads, station_list, station_count, moveout, offset_grid, *tables(length))


def solution(mesh):
    in_specs = (
        P("sta", None, "tpl"),
        P(("tpl", "sta"), None, None, None),
        P(("tpl", "sta"), None),
        P(("tpl", "sta")),
        P(("tpl", "sta"), None),
        P(),
    )
    out_specs = P(("tpl", "sta"), None)
    return jax.shard_map(
        on_device, mesh=mesh, in_specs=in_specs, out_specs=out_specs, check_vma=False
    )
```

time: 467 us -> 55.6 us (0.12)
  local copies, waits for them, and re-layouts: 340 us -> 8.36 us
  Pallas kernels: 0 us -> 46.8 us
  starting transfers between devices: 34.2 us -> 0 us
  other arithmetic: 33 us -> 0 us
  matrix products: 21.1 us -> 0 us
  waiting for transfers between devices: 18.4 us -> 0 us
  blocking collectives: 15.1 us -> 0 us
    gather x9 -> x0, local copies, waits for them, and re-layouts: 313 us -> none  [the longest x3 302 us: stack_all(): taken = jnp.take_along_axis(summed, lag_idx + shifts[:, :, None], axis=2)]
    pallas_call x0 -> x1, Pallas kernels: none -> 46.8 us  [on_device(): pl.pallas_call(functools.partial(kernel, sizes), out_shape=jax.ShapeDtype...]
    all_to_all x2 -> x0, starting transfers between devices: 34.2 us -> none  [the longest x1 19.1 us: on_device(): lax.all_to_all(wanted.reshape(capacity, owners), 'sta', split_axis=1, con...]
    dot_general x17 -> x0, matrix products: 21.1 us -> none  [the longest x4 9.33 us: correlate_rows(): jnp.dot(product.reshape(-1, product.shape[-1]), inverse, preferred_elemen...]
    all_to_all x2 -> x0, waiting for transfers between devices: 18.4 us -> none  [the longest x1 18.4 us: on_device(): lax.all_to_all(flat_window[incoming_ids], 'sta', split_axis=1, concat_axi...]
    another operation x11 -> x0, other arithmetic: 15.6 us -> none
    all_gather x1 -> x0, blocking collectives: 15.1 us -> none  [on_device(): window = lax.all_gather(samples, 'tpl', axis=2, tiled=True)]
    sin x1 -> x0, other arithmetic: 8.88 us -> none  [tables(): sines = jnp.sin(angles)]
  transfers between devices with their start and end apart: 2 -> 0, of which waited for: 1 -> 0; matrix products, arithmetic and copies ran while one was open for 6% -> 0% of each run, Pallas kernels for 0% -> 0%
where the time goes in v1:
time: 55.6 us; the launch traced here: 55.2 us
  Pallas kernels  46.8 us (84%)
  local copies, waits for them, and re-layouts  8.36 us (15%)
    pallas_call x1, Pallas kernels, on_device(): pl.pallas_call(functools.partial(kernel, sizes), out_shape=jax.ShapeDtype...  46.8 us
    unnamed x19, local copies, waits for them, and re-layouts  8.36 us

profile of v1, /device:TPU:1, one launch (start us, length us, event | category | flops | bytes accessed | tf_op | source)
XLA Modules:
  0.0 55.2 jit_solution(4817969770976216526)
XLA Ops:
  0.0 0.0 copy-start
  0.0 0.9 %copy-done = bf16[4,20,3,384]{3,0,2,1:T(4,128)(2,1)S(1)} copy-done((bf16[4,20,3,384]{3,0,2,1:T(4,128)(2,1)S(1)}, bf16[4,20,3,384]{3,0,2,1:T(4,128)(2,1)}, u32[]{:S(2)}) %copy-start) | copy-done | bytes 184344
  0.9 0.0 copy-start.1
  0.9 0.7 %copy-done.1 = bf16[16,3,144]{2,0,1:T(8,128)(2,1)S(1)} copy-done((bf16[16,3,144]{2,0,1:T(8,128)(2,1)S(1)}, bf16[16,3,144]{2,0,1:T(8,128)(2,1)}, u32[]{:S(2)}) %copy-start.1) | copy-done | bytes 13848
  1.7 0.0 copy-start.2
  1.7 0.7 %copy-done.2 = s32[1024]{0:T(1024)S(1)} copy-done((s32[1024]{0:T(1024)S(1)}, s32[1024]{0:T(1024)}, u32[]{:S(2)}) %copy-start.2) | copy-done | bytes 4120
  2.3 0.0 copy-start.3
  2.4 0.7 %copy-done.3 = s32[4,20]{1,0:T(4,128)S(1)} copy-done((s32[4,20]{1,0:T(4,128)S(1)}, s32[4,20]{1,0:T(4,128)}, u32[]{:S(2)}) %copy-start.3) | copy-done | bytes 344
  3.0 0.0 copy-start.4
  3.0 0.7 %copy-done.4 = s32[4,20]{1,0:T(4,128)S(1)} copy-done((s32[4,20]{1,0:T(4,128)S(1)}, s32[4,20]{1,0:T(4,128)}, u32[]{:S(2)}) %copy-start.4) | copy-done | bytes 344
  3.7 0.0 copy-start.5
  3.7 0.7 %copy-done.5 = s32[4]{0:T(128)S(1)} copy-done((s32[4]{0:T(128)S(1)}, s32[4]{0:T(128)}, u32[]{:S(2)}) %copy-start.5) | copy-done | bytes 40
  4.4 0.0 copy-start.6
  4.4 1.3 %copy-done.6 = bf16[768,768]{1,0:T(8,128)(2,1)S(1)} copy-done((bf16[768,768]{1,0:T(8,128)(2,1)S(1)}, bf16[768,768]{1,0:T(8,128)(2,1)}, u32[]{:S(2)}) %copy-start.6) | copy-done | bytes 1179672
  5.6 0.0 copy-start.7
  5.6 1.1 %copy-done.7 = bf16[768,384]{1,0:T(8,128)(2,1)S(1)} copy-done((bf16[768,384]{1,0:T(8,128)(2,1)S(1)}, bf16[768,384]{1,0:T(8,128)(2,1)}, u32[]{:S(2)}) %copy-start.7) | copy-done | bytes 589848
  6.7 0.0 copy-start.8
  6.7 1.1 %copy-done.8 = bf16[768,384]{1,0:T(8,128)(2,1)S(1)} copy-done((bf16[768,384]{1,0:T(8,128)(2,1)S(1)}, bf16[768,384]{1,0:T(8,128)(2,1)}, u32[]{:S(2)}) %copy-start.8) | copy-done | bytes 589848
  7.8 46.8 %shard_map.91 = f32[4,384]{1,0:T(4,128)S(1)} custom-call(bf16[48,144]{1,0:T(8,128)(2,1)S(1)} %bitcast.8, bf16[60,4,384]{2,1,0:T(4,128)(2,1)S(1)} %bitcast.7, s32[4,20]{1,0:T(4,128)S(1)} %copy-done.3, s32[4]{0:T(128)S(1)} %copy-done.5, s32[4,20]{1,0:T(4,128)S(1)} %copy-done.4, s32[8,128]{1,0:T(8,128)S(1)} %bitcast.9, bf16[768,768]{1,0:T(8,128)(2,1)S(1)} %copy-done.6, ...), custom_call_target="tpu_custom_call" | custom-call | flops 2000000000 | bytes 6000000 | tf_op jit(solution)/shard_map/pallas_call | solution.py:389
  54.6 0.6 %copy.11 = f32[4,384]{1,0:T(4,128)} copy(f32[4,384]{1,0:T(4,128)S(1)} %shard_map.91) | data formatting | bytes 12288
Async XLA Ops:
  0.0 0.9 %copy-start = (bf16[4,20,3,384]{3,0,2,1:T(4,128)(2,1)S(1)}, bf16[4,20,3,384]{3,0,2,1:T(4,128)(2,1)}, u32[]{:S(2)}) copy-start(bf16[4,20,3,384]{3,0,2,1:T(4,128)(2,1)} %param.10) | copy-start | bytes 552964
  0.9 0.7 %copy-start.1 = (bf16[16,3,144]{2,0,1:T(8,128)(2,1)S(1)}, bf16[16,3,144]{2,0,1:T(8,128)(2,1)}, u32[]{:S(2)}) copy-start(bf16[16,3,144]{2,0,1:T(8,128)(2,1)} %param.9) | copy-start | bytes 41476
  1.7 0.7 %copy-start.2 = (s32[1024]{0:T(1024)S(1)}, s32[1024]{0:T(1024)}, u32[]{:S(2)}) copy-start(s32[1024]{0:T(1024)} %param.14) | copy-start | bytes 12292
  2.3 0.7 %copy-start.3 = (s32[4,20]{1,0:T(4,128)S(1)}, s32[4,20]{1,0:T(4,128)}, u32[]{:S(2)}) copy-start(s32[4,20]{1,0:T(4,128)} %station_list.1) | copy-start | bytes 964
  3.0 0.7 %copy-start.4 = (s32[4,20]{1,0:T(4,128)S(1)}, s32[4,20]{1,0:T(4,128)}, u32[]{:S(2)}) copy-start(s32[4,20]{1,0:T(4,128)} %moveout.1) | copy-start | bytes 964
  3.7 0.7 %copy-start.5 = (s32[4]{0:T(128)S(1)}, s32[4]{0:T(128)}, u32[]{:S(2)}) copy-start(s32[4]{0:T(128)} %station_count.1) | copy-start | bytes 52
  4.4 1.3 %copy-start.6 = (bf16[768,768]{1,0:T(8,128)(2,1)S(1)}, bf16[768,768]{1,0:T(8,128)(2,1)}, u32[]{:S(2)}) copy-start(bf16[768,768]{1,0:T(8,128)(2,1)} %constant.6.clone.forward_hbm) | copy-start | bytes 3538948
  5.6 1.1 %copy-start.7 = (bf16[768,384]{1,0:T(8,128)(2,1)S(1)}, bf16[768,384]{1,0:T(8,128)(2,1)}, u32[]{:S(2)}) copy-start(bf16[768,384]{1,0:T(8,128)(2,1)} %constant.8.clone.band_hbm) | copy-start | bytes 1769476
  6.7 1.1 %copy-start.8 = (bf16[768,384]{1,0:T(8,128)(2,1)S(1)}, bf16[768,384]{1,0:T(8,128)(2,1)}, u32[]{:S(2)}) copy-start(bf16[768,384]{1,0:T(8,128)(2,1)} %constant.7.clone.inverse_hbm) | copy-start | bytes 1769476

commit v2 on v1

v2 whole, which is shorter than its diff:
```python
import functools
import math

import jax
import jax.numpy as jnp
import numpy as np
from jax import lax
from jax.experimental import pallas as pl
from jax.experimental.pallas import tpu as pltpu
from jax.sharding import PartitionSpec as P

EPSILON = 1e-06
LANES = 128
ROWS = 8
CAPACITY = 2
CHUNKS = 1
MESH = pl.DeviceIdType.MESH
F32 = jnp.float32
BF16 = jnp.bfloat16


def tables(length):
    frame = 2 * length
    time = np.arange(frame)
    odd = 2 * np.arange(length) + 1
    angles = (np.outer(time, odd) % (2 * frame)).astype(np.float64) * (math.pi / frame)
    cosine, sine = np.cos(angles), np.sin(angles)
    forward = np.concatenate([cosine, -sine], axis=1)
    inverse = np.concatenate([cosine[:length].T, -sine[:length].T], axis=0)
    row = np.arange(frame)[:, None]
    col = np.arange(length)[None, :]
    band = (row >= col) & (row < col + length)
    return tuple(jnp.asarray(a.astype(np.float32), BF16) for a in (forward, inverse, band))


def iota(shape, dim):
    return lax.broadcasted_iota(jnp.int32, shape, dim)


def dot(a, b):
    return jnp.dot(a, b, preferred_element_type=F32)


def split(value):
    high = value.astype(BF16)
    return high, (value - high.astype(F32)).astype(BF16)


def third(value):
    return (value * 171) >> 9


def kernel(
    sizes,
    samples,
    templates,
    list_hbm,
    count_hbm,
    moveout_hbm,
    offsets_hbm,
    forward_hbm,
    inverse_hbm,
    band_hbm,
    out,
    forward,
    inverse,
    band,
    raw,
    station_list,
    station_count,
    moveout,
    offsets,
    traces,
    small,
    pick,
    chunk_in,
    chunk_out,
    outbox,
    inbox,
    parts,
    staged,
    replies,
    answers,
    local_sem,
    part_send,
    part_recv,
    box_sem,
    back_sem,
):
    tpl, sta, stations, channels, tpl_dev, width, length, part = sizes
    depth = 2 * tpl
    owners = sta
    frame = 2 * length
    held = stations * channels
    rows_all = owners * ROWS
    slots = CAPACITY * owners
    entries = tpl_dev * width * channels
    columns = (entries + LANES - 1) // LANES * LANES
    span = length // LANES

    p = lax.axis_index("tpl")
    s = lax.axis_index("sta")
    x, z = s // depth, s % depth
    slab, half = z // 2, z % 2
    me = x * depth + 2 * p + half

    def member(i):
        o = lax.rem(me + i, owners)
        return {"tpl": (o % depth) // 2, "sta": (o // depth) * depth + 2 * slab + o % 2}

    def source(i):
        return {"tpl": i, "sta": me}

    def handler(i):
        return {"tpl": slab, "sta": x * depth + 2 * i + half}

    own = jnp.where(s == me, 1, 0)

    barrier = pltpu.get_barrier_semaphore()
    for i in range(tpl):

        @pl.when((s != me) | (p != i))
        def _():
            pl.semaphore_signal(barrier, inc=1, device_id=source(i), device_id_type=MESH)

    def greet(i, carry):
        pl.semaphore_signal(barrier, inc=1, device_id=member(i), device_id_type=MESH)
        return carry

    lax.fori_loop(1, owners, greet, 0)

    def load(n, src, dst):
        copy = pltpu.make_async_copy(src, dst, local_sem.at[n])
        copy.start()
        return copy

    load_chunk = load(8, samples, chunk_in)
    load_list = load(4, list_hbm, station_list)
    load_count = load(5, count_hbm, station_count)
    load_moveout = load(6, moveout_hbm, moveout)
    load_raw = load(0, templates, raw)
    load_offsets = load(7, offsets_hbm, offsets)
    load_forward = load(1, forward_hbm, forward)
    load_inverse = load(3, inverse_hbm, inverse)
    load_band = load(2, band_hbm, band)

    full, rest = part // LANES, part % LANES
    per = LANES // rest
    groups = held // ROWS
    load_chunk.wait()
    chunk = chunk_in[...].astype(F32)
    packed = [chunk[:, j * LANES : (j + 1) * LANES] for j in range(full)]
    for first in range(0, groups, per):
        pieces = [
            chunk[g * ROWS : (g + 1) * ROWS, full * LANES :]
            for g in range(first, min(first + per, groups))
        ]
        if len(pieces) < per:
            pieces.append(jnp.zeros((ROWS, (per - len(pieces)) * rest), F32))
        packed.append(jnp.concatenate(pieces, axis=1))
    chunk_out[...] = jnp.concatenate(packed, axis=0).astype(BF16)

    small[...] = jnp.zeros(small.shape, F32)
    load_list.wait()
    load_count.wait()
    load_moveout.wait()
    stations_here = station_list[...]
    moves = moveout[...]
    small[0:tpl_dev, 0:width] = (stations_here >> 4).astype(F32)
    small[8 : 8 + tpl_dev, 0:width] = (stations_here & 15).astype(F32)
    small[16 : 16 + tpl_dev, 0:width] = (moves >> 1).astype(F32)
    small[24 : 24 + tpl_dev, 0:width] = (moves & 1).astype(F32)
    col = iota((ROWS, columns), 1)
    col_tpl = col & 3
    col_key = third(col >> 2)
    col_chan = (col >> 2) - 3 * col_key
    expand_row = iota((LANES, columns), 0)
    expand_key = third(iota((LANES, columns), 1) >> 2)
    expand = jnp.where(expand_row == expand_key, 1.0, 0.0).astype(BF16)
    spread = dot(small[...].astype(BF16), expand)
    mine = iota((ROWS, columns), 0) == col_tpl

    def flat(i):
        return jnp.sum(jnp.where(mine, spread[8 * i : 8 * i + 8], 0.0), axis=0, keepdims=True)

    owner_of, local_id, move_high, move_low = flat(0), flat(1), flat(2), flat(3)
    used = jnp.zeros((ROWS, columns), jnp.int32)
    for t in range(tpl_dev):
        used = jnp.where(col_tpl == t, station_count[t], used)
    live = (col_key < used) & (col < entries)
    owner_live = jnp.where(live[0:1], owner_of, -1.0)

    row = iota((rows_all, 1), 0)
    row_owner = (((row >> 3) + me) & (owners - 1)).astype(F32)
    q = row & 7
    row_rank = jnp.where(((q >= 3) & (q < 6)) | (q == 7), 1.0, 0.0)
    row_chan = jnp.where(q >= 6, 0, jnp.where(q >= 3, q - 3, q))
    belongs = owner_live == row_owner
    up_row, up_col = iota((columns, columns), 0), iota((columns, columns), 1)
    up_chan = (up_row >> 2) - 3 * third(up_row >> 2)
    up_chan_col = (up_col >> 2) - 3 * third(up_col >> 2)
    earlier = jnp.where((up_row < up_col) & (up_chan == up_chan_col), 1.0, 0.0).astype(BF16)
    before = dot(jnp.where(belongs, 1.0, 0.0).astype(BF16), earlier)
    hot = jnp.where(
        belongs & (before == row_rank) & (col_chan[0:1] == row_chan), 1.0, 0.0
    )
    pick[...] = hot.astype(BF16)

    load_raw.wait()
    quads = raw[...].astype(F32).reshape(width * channels // 2, 2, tpl_dev, length)
    traces[...] = jnp.zeros(traces.shape, F32)
    traces[0 : width * channels // 2, 0:4, :] = quads[:, 0]
    traces[0 : width * channels // 2, 4:8, :] = quads[:, 1]
    placed = dot(pick[...], traces[...].reshape(columns, length).astype(BF16))
    ones = jnp.ones((columns, LANES), BF16)
    notes = jnp.concatenate(
        [dot((hot * v).astype(BF16), ones) for v in (local_id, move_high, move_low)], axis=1
    )
    outbox[...] = (
        jnp.where(q < 6, placed, notes).reshape(owners, ROWS, length).astype(BF16)
    )

    pl.semaphore_wait(barrier, owners - 1 + tpl - own)

    def part_copy(i):
        return pltpu.make_async_remote_copy(
            src_ref=chunk_out,
            dst_ref=parts.at[p],
            send_sem=part_send.at[i],
            recv_sem=part_recv.at[p],
            device_id=handler(i),
            device_id_type=MESH,
        )

    for i in range(tpl):
        remote = (own == 0) | (slab != i)

        @pl.when(remote)
        def _():
            part_copy(i).start()

        @pl.when(jnp.logical_not(remote))
        def _():
            pltpu.make_async_copy(chunk_out, parts.at[p], part_recv.at[p]).start()

    def box_copy(i):
        return pltpu.make_async_remote_copy(
            src_ref=outbox.at[i],
            dst_ref=inbox.at[owners - i],
            send_sem=box_sem.at[0],
            recv_sem=box_sem.at[1],
            device_id=member(i),
            device_id_type=MESH,
        )

    def post(i, carry):
        box_copy(i).start()
        return carry

    keep = pltpu.make_async_copy(outbox.at[0], inbox.at[0], box_sem.at[2])
    keep.start()
    lax.fori_loop(1, owners, post, 0)

    batch = owners // CHUNKS
    order_row = iota((rows_all, 1), 0)
    group, inner = order_row // slots, order_row % slots
    block, rank = inner // (CAPACITY * batch), (inner % (CAPACITY * batch)) // batch
    sender = block * batch + inner % batch
    place = jnp.where(group < channels, group + channels * rank, CAPACITY * channels + rank)
    order = jnp.where(
        iota((rows_all, rows_all), 1) == sender * ROWS + place, 1.0, 0.0
    ).astype(BF16)
    staged[...] = jnp.zeros(staged.shape, F32)
    load_offsets.wait()
    load_forward.wait()
    load_inverse.wait()
    load_band.wait()
    base = me * stations
    offset_row = jnp.sum(
        jnp.where(
            iota(offsets.shape, 0) == base // LANES, offsets[...].astype(F32), 0.0
        ),
        axis=0,
        keepdims=True,
    )

    keep.wait()
    others = pl.ds(1, owners - 1)
    pltpu.make_async_copy(outbox.at[others], inbox.at[others], box_sem.at[1]).wait()
    arrived = inbox[...].astype(F32).reshape(rows_all, length).astype(BF16)
    sorted_rows = dot(order, arrived)
    meta = sorted_rows[channels * slots :]
    lane = iota((slots, LANES), 1)
    ids = meta[:, 0:LANES].astype(jnp.int32)
    offset_hot = jnp.where(lane == ids + base % LANES, offset_row, 0.0).astype(BF16)
    offset_of = dot(offset_hot, jnp.ones((LANES, LANES), BF16))
    shift = (
        2.0 * meta[:, LANES : 2 * LANES] + meta[:, 2 * LANES : 3 * LANES] + offset_of
    ).astype(jnp.int32)
    station_hot = jnp.where(
        iota((slots, stations), 1) == ids[:, :stations], 1.0, 0.0
    ).astype(BF16)
    tracks = sorted_rows[: channels * slots]
    power = jnp.sum(tracks * tracks, axis=1, keepdims=True) * (1.0 / length)
    scale = lax.rsqrt(power + EPSILON)
    tspec = dot(tracks.astype(BF16), forward[0:length, :]).astype(BF16)

    for i in range(tpl):
        pltpu.make_async_copy(chunk_out, parts.at[i], part_recv.at[i]).wait()
    pieces = []
    for i in range(tpl):
        piece = parts[i].astype(F32)
        pieces += [piece[j * held : (j + 1) * held] for j in range(full)]
        tail = []
        for g in range(groups):
            at = full * held + g // per * ROWS
            tail.append(piece[at : at + ROWS, g % per * rest : (g % per + 1) * rest])
        pieces.append(jnp.concatenate(tail, axis=0))
    record = jnp.concatenate(pieces, axis=1)
    blocks = jnp.concatenate([record[:, :frame], record[:, length : length + frame]], axis=0)
    spectra = dot(blocks.astype(BF16), forward[...]).astype(BF16)
    high, low = split(blocks * blocks)
    energy = dot(high, band[...]) + dot(low, band[...])
    norm = (2.0 / (frame * length)) * lax.rsqrt(energy * (1.0 / length) + EPSILON)
    norm_high, norm_low = split(norm)

    def reply_copy(i):
        return pltpu.make_async_remote_copy(
            src_ref=replies.at[i],
            dst_ref=answers.at[owners - i],
            send_sem=back_sem.at[0],
            recv_sem=back_sem.at[1],
            device_id=member(i),
            device_id_type=MESH,
        )

    def answer(i, carry):
        reply_copy(i).start()
        return carry

    count = CAPACITY * batch
    for k in range(CHUNKS):
        here = slice(k * count, (k + 1) * count)
        pairs = [(c, b) for b in range(2) for c in range(channels)]
        products, weights = [], []
        for c, b in pairs:
            at = slice(b * held + c * stations, b * held + (c + 1) * stations)
            mine = slice(c * slots + k * count, c * slots + (k + 1) * count)
            y = tspec[mine].astype(F32)
            y_re, y_im = y[:, :length], y[:, length:]
            data = dot(station_hot[here], spectra[at])
            x_re, x_im = data[:, :length], data[:, length:]
            products.append(
                jnp.concatenate(
                    [y_re * x_re + y_im * x_im, y_re * x_im - y_im * x_re], axis=1
                ).astype(BF16)
            )
            weights.append(
                (dot(station_hot[here], norm_high[at]) + dot(station_hot[here], norm_low[at]))
                * scale[mine]
            )
        lagged = dot(jnp.concatenate(products, axis=0), inverse[...])
        sums = [None, None]
        for n, (c, b) in enumerate(pairs):
            term = lagged[n * count : (n + 1) * count] * weights[n]
            sums[b] = term if c == 0 else sums[b] + term
        tiles = [sums[b][:, j * LANES : (j + 1) * LANES] for b in range(2) for j in range(span)]
        turn, at_lane = shift[here], lane[here]
        for bit in (2, 1):
            chosen = (turn & (bit * LANES)) != 0
            tiles = [
                jnp.where(chosen, tiles[min(i + bit, len(tiles) - 1)], tiles[i])
                for i in range(span + bit)
            ]
        step = LANES // 2
        while step >= 1:
            chosen = (turn & step) != 0
            turned = [pltpu.roll(tile, LANES - step, 1) for tile in tiles]
            inside = at_lane < LANES - step
            after = turned[1:] + turned[-1:]
            tiles = [
                jnp.where(chosen, jnp.where(inside, turned[i], after[i]), tiles[i])
                for i in range(span + 1)
            ]
            step //= 2
        senders = slice(k * batch, (k + 1) * batch)
        for r in range(CAPACITY):
            for j in range(span):
                staged[senders, r * span + j, :] = tiles[j][r * batch : (r + 1) * batch]
        replies[senders] = staged[senders].astype(BF16)
        lax.fori_loop(max(1, k * batch), (k + 1) * batch, answer, 0)
    keep_back = pltpu.make_async_copy(replies.at[0], answers.at[0], back_sem.at[2])
    keep_back.start()

    wide = iota((4 * ROWS, columns), 0)
    wide_col = iota((4 * ROWS, columns), 1)
    of_template = jnp.where((wide & 7) == (wide_col & 3), 1.0, 0.0).astype(BF16)
    weights = lax.dot_general(
        of_template, pick[...], (((1,), (1,)), ((), ())), preferred_element_type=F32
    )
    weight_q = iota((4 * ROWS, rows_all), 1) & 7
    weight_j = iota((4 * ROWS, rows_all), 0) >> 3
    matches = (weight_q < 6) & ((weight_q == weight_j) | (weight_q == weight_j + 3))
    weights = jnp.where(matches & (weight_j < 3), weights, 0.0).astype(BF16)

    keep_back.wait()
    pltpu.make_async_copy(replies.at[others], answers.at[others], back_sem.at[1]).wait()
    stacked = dot(weights, answers[...].astype(F32).reshape(rows_all, LANES).astype(BF16))
    tops = [stacked[ROWS * j : ROWS * (j + 1)] for j in range(span)]
    square = tops[0] * tops[0]
    for top in tops[1:]:
        square = square + top * top
    mean = jnp.sum(square, axis=1, keepdims=True) * (1.0 / length)
    root = lax.rsqrt(mean + EPSILON)
    for j in range(span):
        out[:, j * LANES : (j + 1) * LANES] = (tops[j] * root)[:tpl_dev]

    for i in range(tpl):

        @pl.when((own == 0) | (slab != i))
        def _():
            part_copy(i).wait_send()

    pltpu.make_async_copy(outbox.at[others], inbox.at[others], box_sem.at[0]).wait()
    pltpu.make_async_copy(replies.at[others], answers.at[others], back_sem.at[0]).wait()


def on_device(samples, templates, station_list, station_count, moveout, offsets):
    stations, channels, part = samples.shape
    tpl_dev, width, _, length = templates.shape
    tpl, sta = lax.axis_size("tpl"), lax.axis_size("sta")
    sizes = (tpl, sta, stations, channels, tpl_dev, width, length, part)
    held = stations * channels
    packs = held // ROWS // (LANES // (part % LANES))
    packed = part // LANES * held + ROWS * max(1, packs)
    rows = jnp.transpose(samples, (1, 0, 2)).reshape(channels * stations, part)
    quads = jnp.transpose(templates, (1, 2, 0, 3)).reshape(width * channels, tpl_dev, length)
    offset_grid = offsets.reshape(-1, LANES)
    frame = 2 * length
    entries = tpl_dev * width * channels
    columns = (entries + LANES - 1) // LANES * LANES
    hbm = pl.BlockSpec(memory_space=pltpu.HBM)
    vmem = pl.BlockSpec(memory_space=pltpu.VMEM)
    dma = pltpu.SemaphoreType.DMA
    return pl.pallas_call(
        functools.partial(kernel, sizes),
        out_shape=jax.ShapeDtypeStruct((tpl_dev, length), F32),
        in_specs=[hbm] * 9,
        out_specs=vmem,
        scratch_shapes=[
            pltpu.VMEM((frame, frame), BF16),
            pltpu.VMEM((frame, length), BF16),
            pltpu.VMEM((frame, length), BF16),
            pltpu.VMEM((width * channels, tpl_dev, length), BF16),
            pltpu.VMEM(station_list.shape, jnp.int32),
            pltpu.SMEM(station_count.shape, jnp.int32),
            pltpu.VMEM(moveout.shape, jnp.int32),
            pltpu.VMEM(offset_grid.shape, jnp.int32),
            pltpu.VMEM((columns // ROWS, ROWS, length), F32),
            pltpu.VMEM((4 * ROWS, LANES), F32),
            pltpu.VMEM((sta * ROWS, columns), BF16),
            pltpu.VMEM((held, part), BF16),
            pltpu.VMEM((packed, LANES), BF16),
            pltpu.VMEM((sta, ROWS, length), BF16),
            pltpu.VMEM((sta, ROWS, length), BF16),
            pltpu.VMEM((tpl, packed, LANES), BF16),
            pltpu.VMEM((sta, ROWS, LANES), F32),
            pltpu.VMEM((sta, ROWS, LANES), BF16),
            pltpu.VMEM((sta, ROWS, LANES), BF16),
            dma((9,)),
            dma((tpl,)),
            dma((tpl,)),
            dma((3,)),
            dma((3,)),
        ],
        compiler_params=pltpu.CompilerParams(
            collective_id=0, has_side_effects=True, vmem_limit_bytes=60 * 2**20
        ),
        cost_estimate=pl.CostEstimate(
            flops=2 * 10**9, bytes_accessed=6 * 10**6, transcendentals=10**5
        ),
    )(rows, quads, station_list, station_count, moveout, offset_grid, *tables(length))


def solution(mesh):
    in_specs = (
        P("sta", None, "tpl"),
        P(("tpl", "sta"), None, None, None),
        P(("tpl", "sta"), None),
        P(("tpl", "sta")),
        P(("tpl", "sta"), None),
        P(),
    )
    out_specs = P(("tpl", "sta"), None)
    return jax.shard_map(
        on_device, mesh=mesh, in_specs=in_specs, out_specs=out_specs, check_vma=False
    )
```

time: 55.6 us -> 41.9 us (0.75)
  local copies, waits for them, and re-layouts: 8.36 us -> 1.29 us
  Pallas kernels: 46.8 us -> 40.5 us
    unnamed x19 -> x1, local copies, waits for them, and re-layouts: 8.36 us -> 1.29 us
    pallas_call x1, Pallas kernels: 46.8 us -> 40.5 us  [on_device(): pl.pallas_call(functools.partial(kernel, sizes), out_shape=jax.ShapeDtype...]
where the time goes in v2:
time: 41.9 us; the launch traced here: 41.8 us
  Pallas kernels  40.5 us (97%)
  local copies, waits for them, and re-layouts  1.29 us (3%)
    pallas_call x1, Pallas kernels, on_device(): pl.pallas_call(functools.partial(kernel, sizes), out_shape=jax.ShapeDtype...  40.5 us
    unnamed x1, local copies, waits for them, and re-layouts  1.29 us

profile of v2, /device:TPU:1, one launch (start us, length us, event | category | flops | bytes accessed | tf_op | source)
XLA Modules:
  0.0 41.8 jit_solution(15918294317070402788)
XLA Ops:
  0.0 40.5 %shard_map.91 = f32[4,384]{1,0:T(4,128)} custom-call(bf16[48,144]{1,0:T(8,128)(2,1)} %bitcast.8, bf16[60,4,384]{2,1,0:T(4,128)(2,1)} %bitcast.7, s32[4,20]{1,0:T(4,128)} %list_hbm.1, s32[4]{0:T(128)} %count_hbm.1, s32[4,20]{1,0:T(4,128)} %moveout_hbm.1, s32[8,128]{1,0:T(8,128)} %bitcast.9, bf16[768,768]{1,0:T(8,128)(2,1)} %constant.6.clone.forward_hbm, ...), custom_call_target="tpu_custom_call" | custom-call | flops 2000000000 | bytes 6000000 | tf_op jit(solution)/shard_map/pallas_call | solution.py:445
  40.5 1.3 %copy.11 = f32[4,384]{1,0:T(4,128)} copy(f32[4,384]{1,0:T(4,128)} %shard_map.91) | data formatting | bytes 12288

commit v3 on v2

--- a/solution.py
+++ b/solution.py
@@ -13,7 +13,9 @@
 LANES = 128
 ROWS = 8
 CAPACITY = 2
-CHUNKS = 1
+BOX = 16
+STRIDE = 4
+NEAR = (1, -1, 2, 0)
 MESH = pl.DeviceIdType.MESH
 F32 = jnp.float32
 BF16 = jnp.bfloat16
@@ -75,6 +77,7 @@
     pick,
     chunk_in,
     chunk_out,
+    relay,
     outbox,
     inbox,
     parts,
@@ -84,16 +87,21 @@
     local_sem,
     part_send,
     part_recv,
+    relay_send,
+    relay_recv,
     box_sem,
     back_sem,
 ):
     tpl, sta, stations, channels, tpl_dev, width, length, part = sizes
     depth = 2 * tpl
-    owners = sta
+    peers = sta // 2
+    relays = depth // STRIDE
     frame = 2 * length
     held = stations * channels
-    rows_all = owners * ROWS
-    slots = CAPACITY * owners
+    pair = 2 * stations
+    places = 2 * CAPACITY
+    rows_all = peers * BOX
+    slots = places * peers
     entries = tpl_dev * width * channels
     columns = (entries + LANES - 1) // LANES * LANES
     span = length // LANES
@@ -101,33 +109,42 @@
     p = lax.axis_index("tpl")
     s = lax.axis_index("sta")
     x, z = s // depth, s % depth
-    slab, half = z // 2, z % 2
-    me = x * depth + 2 * p + half
+    me = x * tpl + p
 
     def member(i):
-        o = lax.rem(me + i, owners)
-        return {"tpl": (o % depth) // 2, "sta": (o // depth) * depth + 2 * slab + o % 2}
-
-    def source(i):
-        return {"tpl": i, "sta": me}
-
-    def handler(i):
-        return {"tpl": slab, "sta": x * depth + 2 * i + half}
-
-    own = jnp.where(s == me, 1, 0)
+        d = lax.rem(me + i, peers)
+        return {"tpl": d % tpl, "sta": (d // tpl) * depth + z}
+
+    def plane(i):
+        return x * depth + lax.rem(z + depth + i, depth)
 
     barrier = pltpu.get_barrier_semaphore()
-    for i in range(tpl):
-
-        @pl.when((s != me) | (p != i))
+    for k in range(1, relays):
+        pl.semaphore_signal(
+            barrier,
+            inc=1,
+            device_id={"tpl": p, "sta": plane(-STRIDE * k)},
+            device_id_type=MESH,
+        )
+    for h in range(2):
+        gap = lax.rem(z + depth - 2 * p - h, STRIDE)
+        hop = jnp.where(gap == 3, -1, gap)
+
+        @pl.when(gap != 0)
         def _():
-            pl.semaphore_signal(barrier, inc=1, device_id=source(i), device_id_type=MESH)
+            for i in range(tpl):
+                pl.semaphore_signal(
+                    barrier,
+                    inc=1,
+                    device_id={"tpl": i, "sta": plane(-hop)},
+                    device_id_type=MESH,
+                )
 
     def greet(i, carry):
         pl.semaphore_signal(barrier, inc=1, device_id=member(i), device_id_type=MESH)
         return carry
 
-    lax.fori_loop(1, owners, greet, 0)
+    lax.fori_loop(1, peers, greet, 0)
 
     def load(n, src, dst):
         copy = pltpu.make_async_copy(src, dst, local_sem.at[n])
@@ -191,10 +208,13 @@
     owner_live = jnp.where(live[0:1], owner_of, -1.0)
 
     row = iota((rows_all, 1), 0)
-    row_owner = (((row >> 3) + me) & (owners - 1)).astype(F32)
-    q = row & 7
-    row_rank = jnp.where(((q >= 3) & (q < 6)) | (q == 7), 1.0, 0.0)
-    row_chan = jnp.where(q >= 6, 0, jnp.where(q >= 3, q - 3, q))
+    q = row & (BOX - 1)
+    traced = q < channels * places
+    row_place = jnp.where(traced, third(q), q - channels * places)
+    row_chan = jnp.where(traced, q - channels * row_place, 0)
+    row_rank = (row_place & 1).astype(F32)
+    row_peer = ((row >> 4) + me) & (peers - 1)
+    row_owner = (2 * row_peer + (row_place >> 1)).astype(F32)
     belongs = owner_live == row_owner
     up_row, up_col = iota((columns, columns), 0), iota((columns, columns), 1)
     up_chan = (up_row >> 2) - 3 * third(up_row >> 2)
@@ -217,36 +237,61 @@
         [dot((hot * v).astype(BF16), ones) for v in (local_id, move_high, move_low)], axis=1
     )
     outbox[...] = (
-        jnp.where(q < 6, placed, notes).reshape(owners, ROWS, length).astype(BF16)
-    )
-
-    pl.semaphore_wait(barrier, owners - 1 + tpl - own)
-
-    def part_copy(i):
+        jnp.where(traced, placed, notes).reshape(peers, BOX, length).astype(BF16)
+    )
+
+    pl.semaphore_wait(barrier, peers - 1 + relays - 1 + relays * (len(NEAR) - 1))
+
+    def relay_copy(k):
         return pltpu.make_async_remote_copy(
             src_ref=chunk_out,
-            dst_ref=parts.at[p],
-            send_sem=part_send.at[i],
-            recv_sem=part_recv.at[p],
-            device_id=handler(i),
+            dst_ref=relay.at[k],
+            send_sem=relay_send.at[k],
+            recv_sem=relay_recv.at[k],
+            device_id={"tpl": p, "sta": plane(STRIDE * k)},
             device_id_type=MESH,
         )
 
-    for i in range(tpl):
-        remote = (own == 0) | (slab != i)
-
-        @pl.when(remote)
-        def _():
-            part_copy(i).start()
-
-        @pl.when(jnp.logical_not(remote))
-        def _():
-            pltpu.make_async_copy(chunk_out, parts.at[p], part_recv.at[p]).start()
+    def part_copy(k, n):
+        origin = lax.rem(z + depth - STRIDE * k, depth)
+        return pltpu.make_async_remote_copy(
+            src_ref=relay.at[k] if k else chunk_out,
+            dst_ref=parts.at[(origin % 2) * tpl + p],
+            send_sem=part_send.at[k * len(NEAR) + n],
+            recv_sem=part_recv.at[(origin % 2) * tpl + p],
+            device_id={"tpl": origin // 2, "sta": plane(NEAR[n])},
+            device_id_type=MESH,
+        )
+
+    def stays(k):
+        return lax.rem(z + depth - STRIDE * k, depth) // 2 == p
+
+    def spread_part(k):
+        for n in range(len(NEAR)):
+            if NEAR[n]:
+                part_copy(k, n).start()
+                continue
+
+            @pl.when(jnp.logical_not(stays(k)))
+            def _():
+                part_copy(k, n).start()
+
+            @pl.when(stays(k))
+            def _():
+                origin = lax.rem(z + depth - STRIDE * k, depth)
+                place = (origin % 2) * tpl + p
+                pltpu.make_async_copy(
+                    relay.at[k] if k else chunk_out, parts.at[place], part_recv.at[place]
+                ).start()
+
+    for k in range(1, relays):
+        relay_copy(k).start()
+    spread_part(0)
 
     def box_copy(i):
         return pltpu.make_async_remote_copy(
             src_ref=outbox.at[i],
-            dst_ref=inbox.at[owners - i],
+            dst_ref=inbox.at[peers - i],
             send_sem=box_sem.at[0],
             recv_sem=box_sem.at[1],
             device_id=member(i),
@@ -259,23 +304,24 @@
 
     keep = pltpu.make_async_copy(outbox.at[0], inbox.at[0], box_sem.at[2])
     keep.start()
-    lax.fori_loop(1, owners, post, 0)
-
-    batch = owners // CHUNKS
+    lax.fori_loop(1, peers, post, 0)
+    for k in range(1, relays):
+        relay_copy(k).wait_recv()
+        spread_part(k)
+
     order_row = iota((rows_all, 1), 0)
     group, inner = order_row // slots, order_row % slots
-    block, rank = inner // (CAPACITY * batch), (inner % (CAPACITY * batch)) // batch
-    sender = block * batch + inner % batch
-    place = jnp.where(group < channels, group + channels * rank, CAPACITY * channels + rank)
+    place, sender = inner // peers, inner % peers
+    at_row = jnp.where(group < channels, group + channels * place, channels * places + place)
     order = jnp.where(
-        iota((rows_all, rows_all), 1) == sender * ROWS + place, 1.0, 0.0
+        iota((rows_all, rows_all), 1) == sender * BOX + at_row, 1.0, 0.0
     ).astype(BF16)
     staged[...] = jnp.zeros(staged.shape, F32)
     load_offsets.wait()
     load_forward.wait()
     load_inverse.wait()
     load_band.wait()
-    base = me * stations
+    base = me * pair
     offset_row = jnp.sum(
         jnp.where(
             iota(offsets.shape, 0) == base // LANES, offsets[...].astype(F32), 0.0
@@ -285,39 +331,50 @@
     )
 
     keep.wait()
-    others = pl.ds(1, owners - 1)
+    others = pl.ds(1, peers - 1)
     pltpu.make_async_copy(outbox.at[others], inbox.at[others], box_sem.at[1]).wait()
     arrived = inbox[...].astype(F32).reshape(rows_all, length).astype(BF16)
     sorted_rows = dot(order, arrived)
     meta = sorted_rows[channels * slots :]
     lane = iota((slots, LANES), 1)
-    ids = meta[:, 0:LANES].astype(jnp.int32)
+    block = iota((slots, LANES), 0) // (CAPACITY * peers)
+    ids = meta[:, 0:LANES].astype(jnp.int32) + stations * block
     offset_hot = jnp.where(lane == ids + base % LANES, offset_row, 0.0).astype(BF16)
     offset_of = dot(offset_hot, jnp.ones((LANES, LANES), BF16))
     shift = (
         2.0 * meta[:, LANES : 2 * LANES] + meta[:, 2 * LANES : 3 * LANES] + offset_of
     ).astype(jnp.int32)
     station_hot = jnp.where(
-        iota((slots, stations), 1) == ids[:, :stations], 1.0, 0.0
+        iota((slots, pair), 1) == ids[:, :pair], 1.0, 0.0
     ).astype(BF16)
     tracks = sorted_rows[: channels * slots]
     power = jnp.sum(tracks * tracks, axis=1, keepdims=True) * (1.0 / length)
     scale = lax.rsqrt(power + EPSILON)
     tspec = dot(tracks.astype(BF16), forward[0:length, :]).astype(BF16)
 
-    for i in range(tpl):
+    for i in range(2 * tpl):
         pltpu.make_async_copy(chunk_out, parts.at[i], part_recv.at[i]).wait()
-    pieces = []
-    for i in range(tpl):
-        piece = parts[i].astype(F32)
-        pieces += [piece[j * held : (j + 1) * held] for j in range(full)]
-        tail = []
-        for g in range(groups):
-            at = full * held + g // per * ROWS
-            tail.append(piece[at : at + ROWS, g % per * rest : (g % per + 1) * rest])
-        pieces.append(jnp.concatenate(tail, axis=0))
-    record = jnp.concatenate(pieces, axis=1)
-    blocks = jnp.concatenate([record[:, :frame], record[:, length : length + frame]], axis=0)
+    records = []
+    for h in range(2):
+        pieces = []
+        for i in range(tpl):
+            piece = parts[h * tpl + i].astype(F32)
+            pieces += [piece[j * held : (j + 1) * held] for j in range(full)]
+            tail = []
+            for g in range(groups):
+                at = full * held + g // per * ROWS
+                tail.append(piece[at : at + ROWS, g % per * rest : (g % per + 1) * rest])
+            pieces.append(jnp.concatenate(tail, axis=0))
+        records.append(jnp.concatenate(pieces, axis=1))
+    blocks = jnp.concatenate(
+        [
+            records[h][c * stations : (c + 1) * stations, b * length : b * length + frame]
+            for b in range(2)
+            for c in range(channels)
+            for h in range(2)
+        ],
+        axis=0,
+    )
     spectra = dot(blocks.astype(BF16), forward[...]).astype(BF16)
     high, low = split(blocks * blocks)
     energy = dot(high, band[...]) + dot(low, band[...])
@@ -327,7 +384,7 @@
     def reply_copy(i):
         return pltpu.make_async_remote_copy(
             src_ref=replies.at[i],
-            dst_ref=answers.at[owners - i],
+            dst_ref=answers.at[peers - i],
             send_sem=back_sem.at[0],
             recv_sem=back_sem.at[1],
             device_id=member(i),
@@ -338,57 +395,51 @@
         reply_copy(i).start()
         return carry
 
-    count = CAPACITY * batch
-    for k in range(CHUNKS):
-        here = slice(k * count, (k + 1) * count)
-        pairs = [(c, b) for b in range(2) for c in range(channels)]
-        products, weights = [], []
-        for c, b in pairs:
-            at = slice(b * held + c * stations, b * held + (c + 1) * stations)
-            mine = slice(c * slots + k * count, c * slots + (k + 1) * count)
-            y = tspec[mine].astype(F32)
-            y_re, y_im = y[:, :length], y[:, length:]
-            data = dot(station_hot[here], spectra[at])
-            x_re, x_im = data[:, :length], data[:, length:]
-            products.append(
-                jnp.concatenate(
-                    [y_re * x_re + y_im * x_im, y_re * x_im - y_im * x_re], axis=1
-                ).astype(BF16)
-            )
-            weights.append(
-                (dot(station_hot[here], norm_high[at]) + dot(station_hot[here], norm_low[at]))
-                * scale[mine]
-            )
-        lagged = dot(jnp.concatenate(products, axis=0), inverse[...])
-        sums = [None, None]
-        for n, (c, b) in enumerate(pairs):
-            term = lagged[n * count : (n + 1) * count] * weights[n]
-            sums[b] = term if c == 0 else sums[b] + term
-        tiles = [sums[b][:, j * LANES : (j + 1) * LANES] for b in range(2) for j in range(span)]
-        turn, at_lane = shift[here], lane[here]
-        for bit in (2, 1):
-            chosen = (turn & (bit * LANES)) != 0
-            tiles = [
-                jnp.where(chosen, tiles[min(i + bit, len(tiles) - 1)], tiles[i])
-                for i in range(span + bit)
-            ]
-        step = LANES // 2
-        while step >= 1:
-            chosen = (turn & step) != 0
-            turned = [pltpu.roll(tile, LANES - step, 1) for tile in tiles]
-            inside = at_lane < LANES - step
-            after = turned[1:] + turned[-1:]
-            tiles = [
-                jnp.where(chosen, jnp.where(inside, turned[i], after[i]), tiles[i])
-                for i in range(span + 1)
-            ]
-            step //= 2
-        senders = slice(k * batch, (k + 1) * batch)
-        for r in range(CAPACITY):
-            for j in range(span):
-                staged[senders, r * span + j, :] = tiles[j][r * batch : (r + 1) * batch]
-        replies[senders] = staged[senders].astype(BF16)
-        lax.fori_loop(max(1, k * batch), (k + 1) * batch, answer, 0)
+    pairs = [(c, b) for b in range(2) for c in range(channels)]
+    products, weights = [], []
+    for c, b in pairs:
+        at = slice((b * channels + c) * pair, (b * channels + c + 1) * pair)
+        mine = slice(c * slots, (c + 1) * slots)
+        y = tspec[mine].astype(F32)
+        y_re, y_im = y[:, :length], y[:, length:]
+        data = dot(station_hot, spectra[at])
+        x_re, x_im = data[:, :length], data[:, length:]
+        products.append(
+            jnp.concatenate(
+                [y_re * x_re + y_im * x_im, y_re * x_im - y_im * x_re], axis=1
+            ).astype(BF16)
+        )
+        weights.append(
+            (dot(station_hot, norm_high[at]) + dot(station_hot, norm_low[at])) * scale[mine]
+        )
+    lagged = dot(jnp.concatenate(products, axis=0), inverse[...])
+    sums = [None, None]
+    for n, (c, b) in enumerate(pairs):
+        term = lagged[n * slots : (n + 1) * slots] * weights[n]
+        sums[b] = term if c == 0 else sums[b] + term
+    tiles = [sums[b][:, j * LANES : (j + 1) * LANES] for b in range(2) for j in range(span)]
+    for bit in (2, 1):
+        chosen = (shift & (bit * LANES)) != 0
+        tiles = [
+            jnp.where(chosen, tiles[min(i + bit, len(tiles) - 1)], tiles[i])
+            for i in range(span + bit)
+        ]
+    step = LANES // 2
+    while step >= 1:
+        chosen = (shift & step) != 0
+        turned = [pltpu.roll(tile, LANES - step, 1) for tile in tiles]
+        inside = lane < LANES - step
+        after = turned[1:] + turned[-1:]
+        tiles = [
+            jnp.where(chosen, jnp.where(inside, turned[i], after[i]), tiles[i])
+            for i in range(span + 1)
+        ]
+        step //= 2
+    for i in range(places):
+        for j in range(span):
+            staged[:, i * span + j, :] = tiles[j][i * peers : (i + 1) * peers]
+    replies[...] = staged[...].astype(BF16)
+    lax.fori_loop(1, peers, answer, 0)
     keep_back = pltpu.make_async_copy(replies.at[0], answers.at[0], back_sem.at[2])
     keep_back.start()
 
@@ -398,10 +449,10 @@
     weights = lax.dot_general(
         of_template, pick[...], (((1,), (1,)), ((), ())), preferred_element_type=F32
     )
-    weight_q = iota((4 * ROWS, rows_all), 1) & 7
+    weight_q = iota((4 * ROWS, rows_all), 1) & (BOX - 1)
     weight_j = iota((4 * ROWS, rows_all), 0) >> 3
-    matches = (weight_q < 6) & ((weight_q == weight_j) | (weight_q == weight_j + 3))
-    weights = jnp.where(matches & (weight_j < 3), weights, 0.0).astype(BF16)
+    matches = (weight_q < span * places) & (weight_q - span * third(weight_q) == weight_j)
+    weights = jnp.where(matches, weights, 0.0).astype(BF16)
 
     keep_back.wait()
     pltpu.make_async_copy(replies.at[others], answers.at[others], back_sem.at[1]).wait()
@@ -415,11 +466,17 @@
     for j in range(span):
         out[:, j * LANES : (j + 1) * LANES] = (tops[j] * root)[:tpl_dev]
 
-    for i in range(tpl):
-
-        @pl.when((own == 0) | (slab != i))
-        def _():
-            part_copy(i).wait_send()
+    for k in range(relays):
+        if k:
+            relay_copy(k).wait_send()
+        for n in range(len(NEAR)):
+            if NEAR[n]:
+                part_copy(k, n).wait_send()
+                continue
+
+            @pl.when(jnp.logical_not(stays(k)))
+            def _():
+                part_copy(k, n).wait_send()
 
     pltpu.make_async_copy(outbox.at[others], inbox.at[others], box_sem.at[0]).wait()
     pltpu.make_async_copy(replies.at[others], answers.at[others], back_sem.at[0]).wait()
@@ -431,8 +488,8 @@
     tpl, sta = lax.axis_size("tpl"), lax.axis_size("sta")
     sizes = (tpl, sta, stations, channels, tpl_dev, width, length, part)
     held = stations * channels
-    packs = held // ROWS // (LANES // (part % LANES))
-    packed = part // LANES * held + ROWS * max(1, packs)
+    packs = -(-(held // ROWS) // (LANES // (part % LANES)))
+    packed = part // LANES * held + ROWS * packs
     rows = jnp.transpose(samples, (1, 0, 2)).reshape(channels * stations, part)
     quads = jnp.transpose(templates, (1, 2, 0, 3)).reshape(width * channels, tpl_dev, length)
     offset_grid = offsets.reshape(-1, LANES)
@@ -461,15 +518,18 @@
             pltpu.VMEM((sta * ROWS, columns), BF16),
             pltpu.VMEM((held, part), BF16),
             pltpu.VMEM((packed, LANES), BF16),
-            pltpu.VMEM((sta, ROWS, length), BF16),
-            pltpu.VMEM((sta, ROWS, length), BF16),
-            pltpu.VMEM((tpl, packed, LANES), BF16),
-            pltpu.VMEM((sta, ROWS, LANES), F32),
-            pltpu.VMEM((sta, ROWS, LANES), BF16),
-            pltpu.VMEM((sta, ROWS, LANES), BF16),
+            pltpu.VMEM((2 * tpl // STRIDE, packed, LANES), BF16),
+            pltpu.VMEM((sta // 2, BOX, length), BF16),
+            pltpu.VMEM((sta // 2, BOX, length), BF16),
+            pltpu.VMEM((2 * tpl, packed, LANES), BF16),
+            pltpu.VMEM((sta // 2, BOX, LANES), F32),
+            pltpu.VMEM((sta // 2, BOX, LANES), BF16),
+            pltpu.VMEM((sta // 2, BOX, LANES), BF16),
             dma((9,)),
-            dma((tpl,)),
-            dma((tpl,)),
+            dma((8 * tpl // STRIDE,)),
+            dma((2 * tpl,)),
+            dma((2 * tpl // STRIDE,)),
+            dma((2 * tpl // STRIDE,)),
             dma((3,)),
             dma((3,)),
         ],

time: 41.9 us -> 39.3 us (0.938)
  Pallas kernels: 40.5 us -> 37.8 us
    pallas_call x1, Pallas kernels: 40.5 us -> 37.8 us  [on_device(): pl.pallas_call(functools.partial(kernel, sizes), out_shape=jax.ShapeDtype...]
where the time goes in v3:
time: 39.3 us; the launch traced here: 39.1 us
  Pallas kernels  37.8 us (96%)
  local copies, waits for them, and re-layouts  1.29 us (3%)
    pallas_call x1, Pallas kernels, on_device(): pl.pallas_call(functools.partial(kernel, sizes), out_shape=jax.ShapeDtype...  37.8 us
    unnamed x1, local copies, waits for them, and re-layouts  1.29 us

profile of v3, /device:TPU:1, one launch (start us, length us, event | category | flops | bytes accessed | tf_op | source)
XLA Modules:
  0.0 39.1 jit_solution(5604335447499510573)
XLA Ops:
  0.0 37.8 %shard_map.91 = f32[4,384]{1,0:T(4,128)} custom-call(bf16[48,144]{1,0:T(8,128)(2,1)} %bitcast.8, bf16[60,4,384]{2,1,0:T(4,128)(2,1)} %bitcast.7, s32[4,20]{1,0:T(4,128)} %list_hbm.1, s32[4]{0:T(128)} %count_hbm.1, s32[4,20]{1,0:T(4,128)} %moveout_hbm.1, s32[8,128]{1,0:T(8,128)} %bitcast.9, bf16[768,768]{1,0:T(8,128)(2,1)} %constant.6.clone.forward_hbm, ...), custom_call_target="tpu_custom_call" | custom-call | flops 2000000000 | bytes 6000000 | tf_op jit(solution)/shard_map/pallas_call | solution.py:502
  37.8 1.3 %copy.11 = f32[4,384]{1,0:T(4,128)} copy(f32[4,384]{1,0:T(4,128)} %shard_map.91) | data formatting | bytes 12288

commit v4 on v3

--- a/solution.py
+++ b/solution.py
@@ -15,6 +15,8 @@
 CAPACITY = 2
 BOX = 16
 STRIDE = 4
+SHIFT = 2
+TURN = 13
 NEAR = (1, -1, 2, 0)
 MESH = pl.DeviceIdType.MESH
 F32 = jnp.float32
@@ -115,19 +117,29 @@
         d = lax.rem(me + i, peers)
         return {"tpl": d % tpl, "sta": (d // tpl) * depth + z}
 
+    def far(k):
+        return STRIDE * k + SHIFT
+
     def plane(i):
-        return x * depth + lax.rem(z + depth + i, depth)
+        return x * depth + lax.rem(z + 2 * depth + i, depth)
+
+    def load(n, src, dst):
+        copy = pltpu.make_async_copy(src, dst, local_sem.at[n])
+        copy.start()
+        return copy
+
+    load_chunk = load(8, samples, chunk_in)
 
     barrier = pltpu.get_barrier_semaphore()
-    for k in range(1, relays):
+    for k in range(relays):
         pl.semaphore_signal(
             barrier,
             inc=1,
-            device_id={"tpl": p, "sta": plane(-STRIDE * k)},
+            device_id={"tpl": p, "sta": plane(-far(k))},
             device_id_type=MESH,
         )
     for h in range(2):
-        gap = lax.rem(z + depth - 2 * p - h, STRIDE)
+        gap = lax.rem(z + 2 * depth - SHIFT - 2 * p - h, STRIDE)
         hop = jnp.where(gap == 3, -1, gap)
 
         @pl.when(gap != 0)
@@ -146,12 +158,6 @@
 
     lax.fori_loop(1, peers, greet, 0)
 
-    def load(n, src, dst):
-        copy = pltpu.make_async_copy(src, dst, local_sem.at[n])
-        copy.start()
-        return copy
-
-    load_chunk = load(8, samples, chunk_in)
     load_list = load(4, list_hbm, station_list)
     load_count = load(5, count_hbm, station_count)
     load_moveout = load(6, moveout_hbm, moveout)
@@ -176,6 +182,53 @@
             pieces.append(jnp.zeros((ROWS, (per - len(pieces)) * rest), F32))
         packed.append(jnp.concatenate(pieces, axis=1))
     chunk_out[...] = jnp.concatenate(packed, axis=0).astype(BF16)
+
+    pl.semaphore_wait(barrier, peers - 1 + relays + relays * (len(NEAR) - 1))
+
+    def relay_copy(k):
+        return pltpu.make_async_remote_copy(
+            src_ref=chunk_out,
+            dst_ref=relay.at[k],
+            send_sem=relay_send.at[k],
+            recv_sem=relay_recv.at[k],
+            device_id={"tpl": p, "sta": plane(far(k))},
+            device_id_type=MESH,
+        )
+
+    def part_copy(k, n):
+        origin = lax.rem(z + 2 * depth - far(k), depth)
+        return pltpu.make_async_remote_copy(
+            src_ref=relay.at[k],
+            dst_ref=parts.at[(origin % 2) * tpl + p],
+            send_sem=part_send.at[k * len(NEAR) + n],
+            recv_sem=part_recv.at[(origin % 2) * tpl + p],
+            device_id={"tpl": origin // 2, "sta": plane(NEAR[n])},
+            device_id_type=MESH,
+        )
+
+    def stays(k):
+        return lax.rem(z + 2 * depth - far(k), depth) // 2 == p
+
+    def spread_part(k):
+        for n in range(len(NEAR)):
+            if NEAR[n]:
+                part_copy(k, n).start()
+                continue
+
+            @pl.when(jnp.logical_not(stays(k)))
+            def _():
+                part_copy(k, n).start()
+
+            @pl.when(stays(k))
+            def _():
+                origin = lax.rem(z + 2 * depth - far(k), depth)
+                place = (origin % 2) * tpl + p
+                pltpu.make_async_copy(
+                    relay.at[k], parts.at[place], part_recv.at[place]
+                ).start()
+
+    for k in sorted(range(relays), key=lambda k: -min(far(k), depth - far(k))):
+        relay_copy(k).start()
 
     small[...] = jnp.zeros(small.shape, F32)
     load_list.wait()
@@ -240,54 +293,6 @@
         jnp.where(traced, placed, notes).reshape(peers, BOX, length).astype(BF16)
     )
 
-    pl.semaphore_wait(barrier, peers - 1 + relays - 1 + relays * (len(NEAR) - 1))
-
-    def relay_copy(k):
-        return pltpu.make_async_remote_copy(
-            src_ref=chunk_out,
-            dst_ref=relay.at[k],
-            send_sem=relay_send.at[k],
-            recv_sem=relay_recv.at[k],
-            device_id={"tpl": p, "sta": plane(STRIDE * k)},
-            device_id_type=MESH,
-        )
-
-    def part_copy(k, n):
-        origin = lax.rem(z + depth - STRIDE * k, depth)
-        return pltpu.make_async_remote_copy(
-            src_ref=relay.at[k] if k else chunk_out,
-            dst_ref=parts.at[(origin % 2) * tpl + p],
-            send_sem=part_send.at[k * len(NEAR) + n],
-            recv_sem=part_recv.at[(origin % 2) * tpl + p],
-            device_id={"tpl": origin // 2, "sta": plane(NEAR[n])},
-            device_id_type=MESH,
-        )
-
-    def stays(k):
-        return lax.rem(z + depth - STRIDE * k, depth) // 2 == p
-
-    def spread_part(k):
-        for n in range(len(NEAR)):
-            if NEAR[n]:
-                part_copy(k, n).start()
-                continue
-
-            @pl.when(jnp.logical_not(stays(k)))
-            def _():
-                part_copy(k, n).start()
-
-            @pl.when(stays(k))
-            def _():
-                origin = lax.rem(z + depth - STRIDE * k, depth)
-                place = (origin % 2) * tpl + p
-                pltpu.make_async_copy(
-                    relay.at[k] if k else chunk_out, parts.at[place], part_recv.at[place]
-                ).start()
-
-    for k in range(1, relays):
-        relay_copy(k).start()
-    spread_part(0)
-
     def box_copy(i):
         return pltpu.make_async_remote_copy(
             src_ref=outbox.at[i],
@@ -299,13 +304,13 @@
         )
 
     def post(i, carry):
-        box_copy(i).start()
+        box_copy(lax.rem(i * TURN, peers)).start()
         return carry
 
     keep = pltpu.make_async_copy(outbox.at[0], inbox.at[0], box_sem.at[2])
     keep.start()
     lax.fori_loop(1, peers, post, 0)
-    for k in range(1, relays):
+    for k in sorted(range(relays), key=lambda k: min(far(k), depth - far(k))):
         relay_copy(k).wait_recv()
         spread_part(k)
 
@@ -351,6 +356,17 @@
     power = jnp.sum(tracks * tracks, axis=1, keepdims=True) * (1.0 / length)
     scale = lax.rsqrt(power + EPSILON)
     tspec = dot(tracks.astype(BF16), forward[0:length, :]).astype(BF16)
+
+    wide = iota((4 * ROWS, columns), 0)
+    wide_col = iota((4 * ROWS, columns), 1)
+    of_template = jnp.where((wide & 7) == (wide_col & 3), 1.0, 0.0).astype(BF16)
+    of_rows = lax.dot_general(
+        of_template, pick[...], (((1,), (1,)), ((), ())), preferred_element_type=F32
+    )
+    weight_q = iota((4 * ROWS, rows_all), 1) & (BOX - 1)
+    weight_j = iota((4 * ROWS, rows_all), 0) >> 3
+    matches = (weight_q < span * places) & (weight_q - span * third(weight_q) == weight_j)
+    of_rows = jnp.where(matches, of_rows, 0.0).astype(BF16)
 
     for i in range(2 * tpl):
         pltpu.make_async_copy(chunk_out, parts.at[i], part_recv.at[i]).wait()
@@ -392,7 +408,7 @@
         )
 
     def answer(i, carry):
-        reply_copy(i).start()
+        reply_copy(lax.rem(i * TURN, peers)).start()
         return carry
 
     pairs = [(c, b) for b in range(2) for c in range(channels)]
@@ -443,20 +459,9 @@
     keep_back = pltpu.make_async_copy(replies.at[0], answers.at[0], back_sem.at[2])
     keep_back.start()
 
-    wide = iota((4 * ROWS, columns), 0)
-    wide_col = iota((4 * ROWS, columns), 1)
-    of_template = jnp.where((wide & 7) == (wide_col & 3), 1.0, 0.0).astype(BF16)
-    weights = lax.dot_general(
-        of_template, pick[...], (((1,), (1,)), ((), ())), preferred_element_type=F32
-    )
-    weight_q = iota((4 * ROWS, rows_all), 1) & (BOX - 1)
-    weight_j = iota((4 * ROWS, rows_all), 0) >> 3
-    matches = (weight_q < span * places) & (weight_q - span * third(weight_q) == weight_j)
-    weights = jnp.where(matches, weights, 0.0).astype(BF16)
-
     keep_back.wait()
     pltpu.make_async_copy(replies.at[others], answers.at[others], back_sem.at[1]).wait()
-    stacked = dot(weights, answers[...].astype(F32).reshape(rows_all, LANES).astype(BF16))
+    stacked = dot(of_rows, answers[...].astype(F32).reshape(rows_all, LANES).astype(BF16))
     tops = [stacked[ROWS * j : ROWS * (j + 1)] for j in range(span)]
     square = tops[0] * tops[0]
     for top in tops[1:]:
@@ -467,8 +472,7 @@
         out[:, j * LANES : (j + 1) * LANES] = (tops[j] * root)[:tpl_dev]
 
     for k in range(relays):
-        if k:
-            relay_copy(k).wait_send()
+        relay_copy(k).wait_send()
         for n in range(len(NEAR)):
             if NEAR[n]:
                 part_copy(k, n).wait_send()

time: 39.3 us -> 37.8 us (0.962)
  Pallas kernels: 37.8 us -> 36.4 us
    pallas_call x1, Pallas kernels: 37.8 us -> 36.4 us  [on_device(): pl.pallas_call(functools.partial(kernel, sizes), out_shape=jax.ShapeDtype...]
where the time goes in v4:
time: 37.8 us; the launch traced here: 37.6 us
  Pallas kernels  36.4 us (96%)
  local copies, waits for them, and re-layouts  1.29 us (3%)
    pallas_call x1, Pallas kernels, on_device(): pl.pallas_call(functools.partial(kernel, sizes), out_shape=jax.ShapeDtype...  36.4 us
    unnamed x1, local copies, waits for them, and re-layouts  1.29 us

profile of v4, /device:TPU:1, one launch (start us, length us, event | category | flops | bytes accessed | tf_op | source)
XLA Modules:
  0.0 37.6 jit_solution(1684998632818470847)
XLA Ops:
  0.0 36.4 %shard_map.91 = f32[4,384]{1,0:T(4,128)} custom-call(bf16[48,144]{1,0:T(8,128)(2,1)} %bitcast.8, bf16[60,4,384]{2,1,0:T(4,128)(2,1)} %bitcast.7, s32[4,20]{1,0:T(4,128)} %list_hbm.1, s32[4]{0:T(128)} %count_hbm.1, s32[4,20]{1,0:T(4,128)} %moveout_hbm.1, s32[8,128]{1,0:T(8,128)} %bitcast.9, bf16[768,768]{1,0:T(8,128)(2,1)} %constant.6.clone.forward_hbm, ...), custom_call_target="tpu_custom_call" | custom-call | flops 2000000000 | bytes 6000000 | tf_op jit(solution)/shard_map/pallas_call | solution.py:506
  36.4 1.3 %copy.11 = f32[4,384]{1,0:T(4,128)} copy(f32[4,384]{1,0:T(4,128)} %shard_map.91) | data formatting | bytes 12288

commit v5 on v4

--- a/solution.py
+++ b/solution.py
@@ -14,10 +14,12 @@
 ROWS = 8
 CAPACITY = 2
 BOX = 16
-STRIDE = 4
-SHIFT = 2
 TURN = 13
-NEAR = (1, -1, 2, 0)
+ROUTES = (
+    (4, (4, 3, 2, 1, 0, -1)),
+    (-4, (-3, -2, -1, 0, 1)),
+    (0, (2, -2, 1, -1, 0)),
+)
 MESH = pl.DeviceIdType.MESH
 F32 = jnp.float32
 BF16 = jnp.bfloat16
@@ -43,11 +45,6 @@
 
 def dot(a, b):
     return jnp.dot(a, b, preferred_element_type=F32)
-
-
-def split(value):
-    high = value.astype(BF16)
-    return high, (value - high.astype(F32)).astype(BF16)
 
 
 def third(value):
@@ -97,7 +94,8 @@
     tpl, sta, stations, channels, tpl_dev, width, length, part = sizes
     depth = 2 * tpl
     peers = sta // 2
-    relays = depth // STRIDE
+    hops = [(k, n) for k, (far, near) in enumerate(ROUTES) for n in near]
+    relays = [k for k, (far, near) in enumerate(ROUTES) if far]
     frame = 2 * length
     held = stations * channels
     pair = 2 * stations
@@ -113,12 +111,12 @@
     x, z = s // depth, s % depth
     me = x * tpl + p
 
+    def turn(j):
+        return lax.rem((j + 1) * TURN, peers)
+
     def member(i):
         d = lax.rem(me + i, peers)
         return {"tpl": d % tpl, "sta": (d // tpl) * depth + z}
-
-    def far(k):
-        return STRIDE * k + SHIFT
 
     def plane(i):
         return x * depth + lax.rem(z + 2 * depth + i, depth)
@@ -131,18 +129,20 @@
     load_chunk = load(8, samples, chunk_in)
 
     barrier = pltpu.get_barrier_semaphore()
-    for k in range(relays):
+    for k in relays:
         pl.semaphore_signal(
             barrier,
             inc=1,
-            device_id={"tpl": p, "sta": plane(-far(k))},
+            device_id={"tpl": p, "sta": plane(-ROUTES[k][0])},
             device_id_type=MESH,
         )
     for h in range(2):
-        gap = lax.rem(z + 2 * depth - SHIFT - 2 * p - h, STRIDE)
-        hop = jnp.where(gap == 3, -1, gap)
-
-        @pl.when(gap != 0)
+        gap = lax.rem(z + depth - 2 * p - h, depth)
+        hop = 0
+        for k, n in hops:
+            hop = jnp.where(gap == (ROUTES[k][0] + n) % depth, n, hop)
+
+        @pl.when(hop != 0)
         def _():
             for i in range(tpl):
                 pl.semaphore_signal(
@@ -153,10 +153,12 @@
                 )
 
     def greet(i, carry):
-        pl.semaphore_signal(barrier, inc=1, device_id=member(i), device_id_type=MESH)
+        pl.semaphore_signal(
+            barrier, inc=1, device_id=member(turn(i)), device_id_type=MESH
+        )
         return carry
 
-    lax.fori_loop(1, peers, greet, 0)
+    lax.fori_loop(0, peers - 1, greet, 0)
 
     load_list = load(4, list_hbm, station_list)
     load_count = load(5, count_hbm, station_count)
@@ -183,7 +185,7 @@
         packed.append(jnp.concatenate(pieces, axis=1))
     chunk_out[...] = jnp.concatenate(packed, axis=0).astype(BF16)
 
-    pl.semaphore_wait(barrier, peers - 1 + relays + relays * (len(NEAR) - 1))
+    pl.semaphore_wait(barrier, peers - 1 + len(relays) + sum(n != 0 for k, n in hops))
 
     def relay_copy(k):
         return pltpu.make_async_remote_copy(
@@ -191,27 +193,27 @@
             dst_ref=relay.at[k],
             send_sem=relay_send.at[k],
             recv_sem=relay_recv.at[k],
-            device_id={"tpl": p, "sta": plane(far(k))},
+            device_id={"tpl": p, "sta": plane(ROUTES[k][0])},
             device_id_type=MESH,
         )
 
     def part_copy(k, n):
-        origin = lax.rem(z + 2 * depth - far(k), depth)
+        origin = lax.rem(z + 2 * depth - ROUTES[k][0], depth)
         return pltpu.make_async_remote_copy(
-            src_ref=relay.at[k],
+            src_ref=relay.at[k] if ROUTES[k][0] else chunk_out,
             dst_ref=parts.at[(origin % 2) * tpl + p],
-            send_sem=part_send.at[k * len(NEAR) + n],
+            send_sem=part_send.at[hops.index((k, n))],
             recv_sem=part_recv.at[(origin % 2) * tpl + p],
-            device_id={"tpl": origin // 2, "sta": plane(NEAR[n])},
+            device_id={"tpl": origin // 2, "sta": plane(n)},
             device_id_type=MESH,
         )
 
     def stays(k):
-        return lax.rem(z + 2 * depth - far(k), depth) // 2 == p
+        return lax.rem(z + 2 * depth - ROUTES[k][0], depth) // 2 == p
 
     def spread_part(k):
-        for n in range(len(NEAR)):
-            if NEAR[n]:
+        for n in ROUTES[k][1]:
+            if n:
                 part_copy(k, n).start()
                 continue
 
@@ -221,14 +223,17 @@
 
             @pl.when(stays(k))
             def _():
-                origin = lax.rem(z + 2 * depth - far(k), depth)
+                origin = lax.rem(z + 2 * depth - ROUTES[k][0], depth)
                 place = (origin % 2) * tpl + p
                 pltpu.make_async_copy(
-                    relay.at[k], parts.at[place], part_recv.at[place]
+                    relay.at[k] if ROUTES[k][0] else chunk_out, parts.at[place], part_recv.at[place]
                 ).start()
 
-    for k in sorted(range(relays), key=lambda k: -min(far(k), depth - far(k))):
+    for k in relays:
         relay_copy(k).start()
+    for k in range(len(ROUTES)):
+        if k not in relays:
+            spread_part(k)
 
     small[...] = jnp.zeros(small.shape, F32)
     load_list.wait()
@@ -304,13 +309,13 @@
         )
 
     def post(i, carry):
-        box_copy(lax.rem(i * TURN, peers)).start()
+        box_copy(turn(i)).start()
         return carry
 
     keep = pltpu.make_async_copy(outbox.at[0], inbox.at[0], box_sem.at[2])
     keep.start()
-    lax.fori_loop(1, peers, post, 0)
-    for k in sorted(range(relays), key=lambda k: min(far(k), depth - far(k))):
+    lax.fori_loop(0, peers - 1, post, 0)
+    for k in relays:
         relay_copy(k).wait_recv()
         spread_part(k)
 
@@ -355,7 +360,7 @@
     tracks = sorted_rows[: channels * slots]
     power = jnp.sum(tracks * tracks, axis=1, keepdims=True) * (1.0 / length)
     scale = lax.rsqrt(power + EPSILON)
-    tspec = dot(tracks.astype(BF16), forward[0:length, :]).astype(BF16)
+    tspec = dot(tracks.astype(BF16), forward[0:length, :]) * scale
 
     wide = iota((4 * ROWS, columns), 0)
     wide_col = iota((4 * ROWS, columns), 1)
@@ -392,10 +397,9 @@
         axis=0,
     )
     spectra = dot(blocks.astype(BF16), forward[...]).astype(BF16)
-    high, low = split(blocks * blocks)
-    energy = dot(high, band[...]) + dot(low, band[...])
+    energy = dot((blocks * blocks).astype(BF16), band[...])
     norm = (2.0 / (frame * length)) * lax.rsqrt(energy * (1.0 / length) + EPSILON)
-    norm_high, norm_low = split(norm)
+    norm = norm.astype(BF16)
 
     def reply_copy(i):
         return pltpu.make_async_remote_copy(
@@ -408,7 +412,7 @@
         )
 
     def answer(i, carry):
-        reply_copy(lax.rem(i * TURN, peers)).start()
+        reply_copy(turn(i)).start()
         return carry
 
     pairs = [(c, b) for b in range(2) for c in range(channels)]
@@ -416,7 +420,7 @@
     for c, b in pairs:
         at = slice((b * channels + c) * pair, (b * channels + c + 1) * pair)
         mine = slice(c * slots, (c + 1) * slots)
-        y = tspec[mine].astype(F32)
+        y = tspec[mine]
         y_re, y_im = y[:, :length], y[:, length:]
         data = dot(station_hot, spectra[at])
         x_re, x_im = data[:, :length], data[:, length:]
@@ -425,9 +429,7 @@
                 [y_re * x_re + y_im * x_im, y_re * x_im - y_im * x_re], axis=1
             ).astype(BF16)
         )
-        weights.append(
-            (dot(station_hot, norm_high[at]) + dot(station_hot, norm_low[at])) * scale[mine]
-        )
+        weights.append(dot(station_hot, norm[at]))
     lagged = dot(jnp.concatenate(products, axis=0), inverse[...])
     sums = [None, None]
     for n, (c, b) in enumerate(pairs):
@@ -455,7 +457,7 @@
         for j in range(span):
             staged[:, i * span + j, :] = tiles[j][i * peers : (i + 1) * peers]
     replies[...] = staged[...].astype(BF16)
-    lax.fori_loop(1, peers, answer, 0)
+    lax.fori_loop(0, peers - 1, answer, 0)
     keep_back = pltpu.make_async_copy(replies.at[0], answers.at[0], back_sem.at[2])
     keep_back.start()
 
@@ -469,12 +471,13 @@
     mean = jnp.sum(square, axis=1, keepdims=True) * (1.0 / length)
     root = lax.rsqrt(mean + EPSILON)
     for j in range(span):
-        out[:, j * LANES : (j + 1) * LANES] = (tops[j] * root)[:tpl_dev]
-
-    for k in range(relays):
-        relay_copy(k).wait_send()
-        for n in range(len(NEAR)):
-            if NEAR[n]:
+        out[:, j * LANES : (j + 1) * LANES] = tops[j] * root
+
+    for k in range(len(ROUTES)):
+        if k in relays:
+            relay_copy(k).wait_send()
+        for n in ROUTES[k][1]:
+            if n:
                 part_copy(k, n).wait_send()
                 continue
 
@@ -503,9 +506,9 @@
     hbm = pl.BlockSpec(memory_space=pltpu.HBM)
     vmem = pl.BlockSpec(memory_space=pltpu.VMEM)
     dma = pltpu.SemaphoreType.DMA
-    return pl.pallas_call(
+    scaled = pl.pallas_call(
         functools.partial(kernel, sizes),
-        out_shape=jax.ShapeDtypeStruct((tpl_dev, length), F32),
+        out_shape=jax.ShapeDtypeStruct((ROWS, length), F32),
         in_specs=[hbm] * 9,
         out_specs=vmem,
         scratch_shapes=[
@@ -522,7 +525,7 @@
             pltpu.VMEM((sta * ROWS, columns), BF16),
             pltpu.VMEM((held, part), BF16),
             pltpu.VMEM((packed, LANES), BF16),
-            pltpu.VMEM((2 * tpl // STRIDE, packed, LANES), BF16),
+            pltpu.VMEM((len(ROUTES), packed, LANES), BF16),
             pltpu.VMEM((sta // 2, BOX, length), BF16),
             pltpu.VMEM((sta // 2, BOX, length), BF16),
             pltpu.VMEM((2 * tpl, packed, LANES), BF16),
@@ -530,10 +533,10 @@
             pltpu.VMEM((sta // 2, BOX, LANES), BF16),
             pltpu.VMEM((sta // 2, BOX, LANES), BF16),
             dma((9,)),
-            dma((8 * tpl // STRIDE,)),
             dma((2 * tpl,)),
-            dma((2 * tpl // STRIDE,)),
-            dma((2 * tpl // STRIDE,)),
+            dma((2 * tpl,)),
+            dma((len(ROUTES),)),
+            dma((len(ROUTES),)),
             dma((3,)),
             dma((3,)),
         ],
@@ -544,6 +547,7 @@
             flops=2 * 10**9, bytes_accessed=6 * 10**6, transcendentals=10**5
         ),
     )(rows, quads, station_list, station_count, moveout, offset_grid, *tables(length))
+    return scaled[:tpl_dev]
 
 
 def solution(mesh):

time: 37.8 us -> 37.7 us (level)
    slice x0 -> x1, local copies, waits for them, and re-layouts: none -> 1.3 us  [on_device(): return scaled[:tpl_dev]]
    unnamed x1 -> x0, local copies, waits for them, and re-layouts: 1.29 us -> none
where the time goes in v5:
time: 37.7 us; the launch traced here: 37.6 us
  Pallas kernels  36.2 us (96%)
  local copies, waits for them, and re-layouts  1.3 us (3%)
    pallas_call x1, Pallas kernels, on_device(): pl.pallas_call(functools.partial(kernel, sizes), out_shape=jax.ShapeDtype...  36.2 us
    slice x1, local copies, waits for them, and re-layouts, on_device(): return scaled[:tpl_dev]  1.3 us

profile of v5, /device:TPU:1, one launch (start us, length us, event | category | flops | bytes accessed | tf_op | source)
XLA Modules:
  0.0 37.6 jit_solution(6895667563716038058)
XLA Ops:
  0.0 36.2 %shard_map.91 = f32[8,384]{1,0:T(8,128)} custom-call(bf16[48,144]{1,0:T(8,128)(2,1)} %bitcast.8, bf16[60,4,384]{2,1,0:T(4,128)(2,1)} %bitcast.7, s32[4,20]{1,0:T(4,128)} %list_hbm.1, s32[4]{0:T(128)} %count_hbm.1, s32[4,20]{1,0:T(4,128)} %moveout_hbm.1, s32[8,128]{1,0:T(8,128)} %bitcast.9, bf16[768,768]{1,0:T(8,128)(2,1)} %constant.6.clone.forward_hbm, ...), custom_call_target="tpu_custom_call" | custom-call | flops 2000000000 | bytes 6000000 | tf_op jit(solution)/shard_map/pallas_call | solution.py:509
  36.2 1.3 %slice.3 = f32[4,384]{1,0:T(4,128)} slice(f32[8,384]{1,0:T(8,128)} %shard_map.91), slice={[0:4], [0:384]} | slice | bytes 12288 | tf_op jit(solution)/shard_map/slice | solution.py:550

commit v6 on v5

--- a/solution.py
+++ b/solution.py
@@ -15,11 +15,7 @@
 CAPACITY = 2
 BOX = 16
 TURN = 13
-ROUTES = (
-    (4, (4, 3, 2, 1, 0, -1)),
-    (-4, (-3, -2, -1, 0, 1)),
-    (0, (2, -2, 1, -1, 0)),
-)
+ROUTES = ((5, (3, 2, 1, 0, -1, -2)), (-5, (-2, -1, 0, 1, 2)), (0, (2, -2, 1, -1, 0)))
 MESH = pl.DeviceIdType.MESH
 F32 = jnp.float32
 BF16 = jnp.bfloat16
@@ -108,15 +104,15 @@
 
     p = lax.axis_index("tpl")
     s = lax.axis_index("sta")
-    x, z = s // depth, s % depth
+    x, z = lax.div(s, depth), lax.rem(s, depth)
     me = x * tpl + p
 
     def turn(j):
-        return lax.rem((j + 1) * TURN, peers)
+        return (j + 1) * TURN % peers
 
     def member(i):
         d = lax.rem(me + i, peers)
-        return {"tpl": d % tpl, "sta": (d // tpl) * depth + z}
+        return {"tpl": lax.rem(d, tpl), "sta": lax.div(d, tpl) * depth + z}
 
     def plane(i):
         return x * depth + lax.rem(z + 2 * depth + i, depth)
@@ -158,7 +154,8 @@
         )
         return carry
 
-    lax.fori_loop(0, peers - 1, greet, 0)
+    for j in range(peers - 1):
+        greet(j, 0)
 
     load_list = load(4, list_hbm, station_list)
     load_count = load(5, count_hbm, station_count)
@@ -201,10 +198,10 @@
         origin = lax.rem(z + 2 * depth - ROUTES[k][0], depth)
         return pltpu.make_async_remote_copy(
             src_ref=relay.at[k] if ROUTES[k][0] else chunk_out,
-            dst_ref=parts.at[(origin % 2) * tpl + p],
+            dst_ref=parts.at[lax.rem(origin, 2) * tpl + p],
             send_sem=part_send.at[hops.index((k, n))],
-            recv_sem=part_recv.at[(origin % 2) * tpl + p],
-            device_id={"tpl": origin // 2, "sta": plane(n)},
+            recv_sem=part_recv.at[lax.rem(origin, 2) * tpl + p],
+            device_id={"tpl": lax.div(origin, 2), "sta": plane(n)},
             device_id_type=MESH,
         )
 
@@ -224,7 +221,7 @@
             @pl.when(stays(k))
             def _():
                 origin = lax.rem(z + 2 * depth - ROUTES[k][0], depth)
-                place = (origin % 2) * tpl + p
+                place = lax.rem(origin, 2) * tpl + p
                 pltpu.make_async_copy(
                     relay.at[k] if ROUTES[k][0] else chunk_out, parts.at[place], part_recv.at[place]
                 ).start()
@@ -457,7 +454,8 @@
         for j in range(span):
             staged[:, i * span + j, :] = tiles[j][i * peers : (i + 1) * peers]
     replies[...] = staged[...].astype(BF16)
-    lax.fori_loop(0, peers - 1, answer, 0)
+    for j in range(peers - 1):
+        answer(j, 0)
     keep_back = pltpu.make_async_copy(replies.at[0], answers.at[0], back_sem.at[2])
     keep_back.start()
 

time: 37.7 us -> 36.9 us (0.979)
  Pallas kernels: 36.2 us -> 35.4 us
    pallas_call x1, Pallas kernels: 36.2 us -> 35.4 us  [on_device(): pl.pallas_call(functools.partial(kernel, sizes), out_shape=jax.ShapeDtype...]
where the time goes in v6:
time: 36.9 us; the launch traced here: 36.7 us
  Pallas kernels  35.4 us (96%)
  local copies, waits for them, and re-layouts  1.3 us (4%)
    pallas_call x1, Pallas kernels, on_device(): pl.pallas_call(functools.partial(kernel, sizes), out_shape=jax.ShapeDtype...  35.4 us
    slice x1, local copies, waits for them, and re-layouts, on_device(): return scaled[:tpl_dev]  1.3 us

profile of v6, /device:TPU:1, one launch (start us, length us, event | category | flops | bytes accessed | tf_op | source)
XLA Modules:
  0.0 36.7 jit_solution(16958012543313712878)
XLA Ops:
  0.0 35.4 %shard_map.91 = f32[8,384]{1,0:T(8,128)} custom-call(bf16[48,144]{1,0:T(8,128)(2,1)} %bitcast.8, bf16[60,4,384]{2,1,0:T(4,128)(2,1)} %bitcast.7, s32[4,20]{1,0:T(4,128)} %list_hbm.1, s32[4]{0:T(128)} %count_hbm.1, s32[4,20]{1,0:T(4,128)} %moveout_hbm.1, s32[8,128]{1,0:T(8,128)} %bitcast.9, bf16[768,768]{1,0:T(8,128)(2,1)} %constant.6.clone.forward_hbm, ...), custom_call_target="tpu_custom_call" | custom-call | flops 2000000000 | bytes 6000000 | tf_op jit(solution)/shard_map/pallas_call | solution.py:507
  35.4 1.3 %slice.3 = f32[4,384]{1,0:T(4,128)} slice(f32[8,384]{1,0:T(8,128)} %shard_map.91), slice={[0:4], [0:384]} | slice | bytes 12288 | tf_op jit(solution)/shard_map/slice | solution.py:548

commit v7 on v6

--- a/solution.py
+++ b/solution.py
@@ -311,7 +311,8 @@
 
     keep = pltpu.make_async_copy(outbox.at[0], inbox.at[0], box_sem.at[2])
     keep.start()
-    lax.fori_loop(0, peers - 1, post, 0)
+    for j in range(peers - 1):
+        post(j, 0)
     for k in relays:
         relay_copy(k).wait_recv()
         spread_part(k)

time: 36.9 us -> 36.9 us (level)
  no operation moved by 1% of the time
where the time goes in v7:
time: 36.9 us; the launch traced here: 36.7 us
  Pallas kernels  35.4 us (96%)
  local copies, waits for them, and re-layouts  1.3 us (4%)
    pallas_call x1, Pallas kernels, on_device(): pl.pallas_call(functools.partial(kernel, sizes), out_shape=jax.ShapeDtype...  35.4 us
    slice x1, local copies, waits for them, and re-layouts, on_device(): return scaled[:tpl_dev]  1.3 us

profile of v7, /device:TPU:1, one launch (start us, length us, event | category | flops | bytes accessed | tf_op | source)
XLA Modules:
  0.0 36.7 jit_solution(17480477798605189882)
XLA Ops:
  0.0 35.4 %shard_map.91 = f32[8,384]{1,0:T(8,128)} custom-call(bf16[48,144]{1,0:T(8,128)(2,1)} %bitcast.8, bf16[60,4,384]{2,1,0:T(4,128)(2,1)} %bitcast.7, s32[4,20]{1,0:T(4,128)} %list_hbm.1, s32[4]{0:T(128)} %count_hbm.1, s32[4,20]{1,0:T(4,128)} %moveout_hbm.1, s32[8,128]{1,0:T(8,128)} %bitcast.9, bf16[768,768]{1,0:T(8,128)(2,1)} %constant.6.clone.forward_hbm, ...), custom_call_target="tpu_custom_call" | custom-call | flops 2000000000 | bytes 6000000 | tf_op jit(solution)/shard_map/pallas_call | solution.py:508
  35.4 1.3 %slice.3 = f32[4,384]{1,0:T(4,128)} slice(f32[8,384]{1,0:T(8,128)} %shard_map.91), slice={[0:4], [0:384]} | slice | bytes 12288 | tf_op jit(solution)/shard_map/slice | solution.py:549

commit v8 on v7

--- a/solution.py
+++ b/solution.py
@@ -15,7 +15,7 @@
 CAPACITY = 2
 BOX = 16
 TURN = 13
-ROUTES = ((5, (3, 2, 1, 0, -1, -2)), (-5, (-2, -1, 0, 1, 2)), (0, (2, -2, 1, -1, 0)))
+ROUTES = ((4, (4, 3, 2, 1, 0, -1)), (-4, (-3, -2, -1, 0, 1)), (0, (2, -2, 1, -1, 0)))
 MESH = pl.DeviceIdType.MESH
 F32 = jnp.float32
 BF16 = jnp.bfloat16

time: 36.9 us -> 37.1 us (level)
  no operation moved by 1% of the time
where the time goes in v8:
time: 37.1 us; the launch traced here: 36.8 us
  Pallas kernels  35.5 us (96%)
  local copies, waits for them, and re-layouts  1.3 us (4%)
    pallas_call x1, Pallas kernels, on_device(): pl.pallas_call(functools.partial(kernel, sizes), out_shape=jax.ShapeDtype...  35.5 us
    slice x1, local copies, waits for them, and re-layouts, on_device(): return scaled[:tpl_dev]  1.3 us

profile of v8, /device:TPU:1, one launch (start us, length us, event | category | flops | bytes accessed | tf_op | source)
XLA Modules:
  0.0 36.8 jit_solution(11713669050353817523)
XLA Ops:
  0.0 35.5 %shard_map.91 = f32[8,384]{1,0:T(8,128)} custom-call(bf16[48,144]{1,0:T(8,128)(2,1)} %bitcast.8, bf16[60,4,384]{2,1,0:T(4,128)(2,1)} %bitcast.7, s32[4,20]{1,0:T(4,128)} %list_hbm.1, s32[4]{0:T(128)} %count_hbm.1, s32[4,20]{1,0:T(4,128)} %moveout_hbm.1, s32[8,128]{1,0:T(8,128)} %bitcast.9, bf16[768,768]{1,0:T(8,128)(2,1)} %constant.6.clone.forward_hbm, ...), custom_call_target="tpu_custom_call" | custom-call | flops 2000000000 | bytes 6000000 | tf_op jit(solution)/shard_map/pallas_call | solution.py:508
  35.5 1.3 %slice.3 = f32[4,384]{1,0:T(4,128)} slice(f32[8,384]{1,0:T(8,128)} %shard_map.91), slice={[0:4], [0:384]} | slice | bytes 12288 | tf_op jit(solution)/shard_map/slice | solution.py:549
